TPU v7x, 32 devices: a whole 2x2x4 slice. The times are simulated.
32 devices in a mesh: ex: 8 (over z, x), feat: 4 (over y, core).
Axes of the slice: x: 2, y: 2, z: 4, core: 2. Of those that a mesh axis runs over, the one named last changes fastest.
Arguments:
- pooled: bfloat16 [16384, 8192], P('ex', 'feat'), may hold values from -6 to 6
- labels: int32 [16384], P('ex'), may hold values from 0 to 1
- sign_bits: int32 [16384], P('ex'), may hold values from 0 to 1
- margins_old: float32 [16384], P('ex'), may hold values from -8 to 8
- direction: float32 [8192], P(('feat', 'ex')), may hold values from -0.0625 to 0.0625
- sample_rows: int32 [1024], replicated, may hold values from 0 to 16383
Outputs:
- margins: float32 [16384], P('ex')
- gradient: float32 [8192], P(('feat', 'ex'))
- sketch: float32 [1024, 8192], P('ex', 'feat')
Inputs may be any that keep to these rules, and one draw needn't show every extreme that they name: `sample_rows`: indices are drawn independently, repeats possible.
All inputs are finite; a program needn't handle non-finite values.
Results may differ from a plain program's by a relative error of at most 0.0033.
Values may be sent and summed in bfloat16 or wider, within the bound.
No kernel may reach another device: no remote copies, remote signals or barrier semaphores. Data moves between devices by JAX's collectives and lax.ppermute only.
A program may use at most 64 MiB of HBM per device.

v0:
```python
import math

import jax
import jax.numpy as jnp
from jax import lax
from jax.sharding import PartitionSpec as P


def parity_table(row_ids, col_ids):
    folded = jnp.bitwise_and(row_ids[:, None], col_ids[None, :])
    for shift_by in (16, 8, 4, 2, 1):
        folded = jnp.bitwise_xor(folded, jnp.right_shift(folded, shift_by))
    odd_bit = jnp.bitwise_and(folded, 1)
    return (1 - 2 * odd_bit).astype(jnp.bfloat16)


def response(margins, labels):
    residual = jax.nn.sigmoid(margins) - labels.astype(jnp.float32)
    weight = jnp.sqrt(jax.nn.sigmoid(margins) * jax.nn.sigmoid(-margins))
    return (residual, weight)


def on_device(pooled, labels, sign_bits, margins_old, direction, sample_rows):
    row_count = pooled.shape[0]
    ex_count = lax.axis_size("ex")
    total_rows = row_count * ex_count
    ex_index = lax.axis_index("ex")
    pieces = lax.all_gather(direction.astype(jnp.bfloat16), "ex", axis=0, tiled=True)
    partial_margins = jnp.dot(pooled, pieces, preferred_element_type=jnp.float32)
    margins = margins_old + lax.psum(partial_margins, "feat")
    residual, weight = response(margins, labels)
    residual_b = residual.astype(jnp.bfloat16)
    gradient = lax.psum_scatter(
        jnp.dot(residual_b, pooled, preferred_element_type=jnp.float32),
        "ex",
        scatter_dimension=0,
        tiled=True,
    ) / math.sqrt(total_rows)
    scale_rows = (2 * sign_bits - 1).astype(jnp.float32) * weight
    weighted = (pooled * scale_rows[:, None]).astype(jnp.bfloat16)
    sketch_count = sample_rows.shape[0]
    col_ids = ex_index * row_count + jnp.arange(row_count, dtype=jnp.int32)
    signs_table = parity_table(sample_rows, col_ids)
    sketch = lax.psum_scatter(
        jnp.dot(signs_table, weighted, preferred_element_type=jnp.float32),
        "ex",
        scatter_dimension=0,
        tiled=True,
    ) / math.sqrt(sketch_count)
    return (margins, gradient, sketch)


def solution(mesh):
    return jax.shard_map(
        on_device,
        mesh=mesh,
        in_specs=(P("ex", "feat"), P("ex"), P("ex"), P("ex"), P(("feat", "ex")), P()),
        out_specs=(P("ex"), P(("feat", "ex")), P("ex", "feat")),
        check_vma=False,
    )
```

profile of v0, /device:TPU:0, one launch (start us, length us, event | category | flops | bytes accessed | tf_op | source)
XLA Modules:
  0.0 216.0 jit_solution(2678253922462588776)
XLA Ops:
  7.2 0.0 copy-start.2
  7.2 0.0 copy-start.1
  7.2 0.0 copy-start.4
  7.2 0.0 reduce-scatter.2.cloned.1.call-start
  7.2 0.7 convert_element_type.21
  7.9 22.2 %all-gather = bf16[8,1,256]{2,1,0:T(2,128)(2,1)S(1)} all-gather(bf16[1,1,256]{2,1,0:T(2,128)(2,1)S(1)} %reshape.12), channel_id=1, replica_groups=mesh['ex'=8,'feat'=4] {'ex'}, dimensions={0}, use_global_device_ids=true | all-gather | bytes 4608 | tf_op jit(solution)/shard_map/all_gather | solution.py:28
  30.2 5.6 %fusion.19 = f32[1,2048]{1,0:T(1,128)S(1)} fusion(bf16[2048,2048]{1,0:T(8,128)(2,1)} %param.6, bf16[2048,1]{0,1:T(2,128)(2,1)S(1)} %bitcast.9), kind=kOutput, calls=%fused_computation.30 | convolution fusion | flops 8388608 | bytes 8400896 | tf_op jit(solution)/shard_map/dot_general | solution.py:29
  35.8 5.8 %psum.7 = f32[2048]{0:T(1024)S(1)} all-reduce(f32[2048]{0:T(1024)S(1)} %bitcast.8), channel_id=1, replica_groups=mesh['ex'=8,'feat'=4] {'feat'}, use_global_device_ids=true, to_apply=%region_0.0 | all-reduce | flops 2048 | bytes 16384 | tf_op jit(solution)/shard_map/psum | solution.py:30
  41.6 0.0 copy-done.2
  41.6 0.0 copy-done.1
  41.6 0.0 copy-start
  41.6 0.0 copy-done.4
  41.6 17.9 %fusion.3 = f32[1024,2048]{1,0:T(8,128)} fusion(bf16[2048,2048]{1,0:T(8,128)(2,1)} %param.6, f32[2048]{0:T(1024)S(1)} %get-tuple-element.3, s32[2048]{0:T(1024)S(1)} %iota_add_fusion, s32[1024]{0:T(1024)S(1)} %copy-done.4), kind=kOutput, calls=%fused_computation.9 | convolution fusion | flops 8633974784 | bytes 16797696 | tf_op jit(solution)/shard_map/dot_general | solution.py:45
  59.6 0.0 copy-start.3
  59.6 0.0 reduce-scatter.2.cloned.1.call-update
  59.6 0.0 copy-done
  59.6 0.7 copy-done.3
  60.3 0.0 copy-done.5
  60.3 0.6 dynamic-slice
  61.5 5.1 %fusion.20 = f32[1,2048]{1,0:T(1,128)S(1)} fusion(bf16[2048,1]{0,1:T(2,128)(2,1)S(1)} %reshape.16, bf16[2048,2048]{1,0:T(8,128)(2,1)} %param.6), kind=kOutput, calls=%fused_computation.31 | convolution fusion | flops 8388608 | bytes 8400896 | tf_op jit(solution)/shard_map/dot_general | solution.py:34
  66.6 18.7 %all-reduce = f32[2048]{0:T(1024)S(1)} all-reduce(f32[2048]{0:T(1024)S(1)} %bitcast.10), channel_id=2, replica_groups=mesh['ex'=8,'feat'=4] {'ex'}, use_global_device_ids=true, to_apply=%region_1.0.clone | all-reduce | flops 2048 | bytes 16384
  85.4 0.6 dynamic-slice_multiply_fusion
  86.0 120.8 %reduce-scatter.2.cloned.1.call-done = f32[128,2048]{1,0:T(8,128)} async-done(((f32[1024,2048]{1,0:T(8,128)}), f32[128,2048]{1,0:T(8,128)}) %reduce-scatter.2.cloned.1.call-update) | async-done | bytes 1048592 | tf_op jit(solution)/shard_map/reduce_scatter | solution.py:44
  206.8 2.3 %broadcast_multiply_fusion = f32[128,2048]{1,0:T(8,128)} fusion(f32[128,2048]{1,0:T(8,128)} %reduce-scatter.2.cloned.1.call-done), kind=kLoop, calls=%fused_computation.19 | loop fusion | flops 262144 | bytes 2097152 | tf_op jit(solution)/shard_map/div | solution.py:44
  (6 shorter events, 0.1 us)
Async XLA Ops:
  7.2 34.4 %copy-start.2 = (f32[2048]{0:T(1024)S(1)}, f32[2048]{0:T(1024)}, u32[]{:S(2)}) copy-start(f32[2048]{0:T(1024)} %param.9) | copy-start | bytes 24580
  7.2 34.4 %copy-start.1 = (s32[2048]{0:T(1024)S(1)}, s32[2048]{0:T(1024)}, u32[]{:S(2)}) copy-start(s32[2048]{0:T(1024)} %param.8) | copy-start | bytes 24580
  7.2 34.5 %copy-start.4 = (s32[1024]{0:T(1024)S(1)}, s32[1024]{0:T(1024)}, u32[]{:S(2)}) copy-start(s32[1024]{0:T(1024)} %param.11) | copy-start | bytes 12292
  7.2 199.6 %reduce-scatter.2.cloned.1.call-start = ((), (), s32[]{:S(2)}) async-start(), calls=%async_computation.1 | async-start | bytes 9437184 | tf_op jit(solution)/shard_map/reduce_scatter | solution.py:44
  41.6 18.0 %copy-start = (f32[2048]{0:T(1024)}, f32[2048]{0:T(1024)S(1)}, u32[]{:S(2)}) copy-start(f32[2048]{0:T(1024)S(1)} %get-tuple-element.4) | copy-start | bytes 24580
  59.6 0.7 copy-start.3
  59.6 0.7 copy-start.5
Sparse Core Ops, SparseCore 0:
  59.7 147.0 reduce-scatter.1
where the time goes:
time: 216 us
  waiting for transfers between devices  121 us (56%)
  blocking collectives  46.7 us (22%)
  matrix products  28.6 us (13%)
  between operations  14.8 us (7%)
  other arithmetic  3.65 us (2%)
    reduce_scatter x1, waiting for transfers between devices, on_device(): lax.psum_scatter(jnp.dot(signs_table, weighted, preferred_element_type=jn...  121 us
    all_gather x1, blocking collectives, on_device(): lax.all_gather(direction.astype(jnp.bfloat16), 'ex', axis=0, tiled=True)  22.2 us
    unnamed x1, blocking collectives  18.7 us
    dot_general x1, matrix products, on_device(): jnp.dot(signs_table, weighted, preferred_element_type=jnp.float32)  17.9 us
    psum x1, blocking collectives, on_device(): margins = margins_old + lax.psum(partial_margins, 'feat')  5.75 us
    dot_general x1, matrix products, on_device(): jnp.dot(pooled, pieces, preferred_element_type=jnp.float32)  5.64 us
    dot_general x1, matrix products, on_device(): jnp.dot(residual_b, pooled, preferred_element_type=jnp.float32)  5.08 us
  transfers between devices with their start and end apart: 1, of which 1 were waited for; matrix products, arithmetic and copies ran while one was open for 3% of the time, Pallas kernels for 0%

commit v1 on v0

v1 whole, which is shorter than its diff:
```python
import functools
import math

import jax
import jax.numpy as jnp
from jax import lax
from jax.experimental import pallas as pl
from jax.experimental.pallas import tpu as pltpu
from jax.sharding import PartitionSpec as P

LANES = 128
VMEM_LIMIT = 48 * 1024 * 1024
PARAMS = pltpu.CompilerParams(vmem_limit_bytes=VMEM_LIMIT)


def tile_of(extent, most):
    size = most
    while extent % size:
        size //= 2
    return size


def swap_with(value, axis, distance):
    count = lax.axis_size(axis)
    return lax.ppermute(value, axis, [(i, i ^ distance) for i in range(count)])


def send_order(bits):
    rounds = []
    for bit in range(bits):
        blocks = [r for r in range(1 << bits) if r & ((2 << bit) - 1) == 1 << bit]
        blocks.sort(key=lambda r: [-(r >> b & 1) for b in range(bit + 1, bits)])
        rounds.append(blocks)
    return rounds


def margins_kernel(dir_ref, pooled_ref, out_ref):
    row = lax.dot_general(
        dir_ref[...], pooled_ref[...], (((1,), (1,)), ((), ())), preferred_element_type=jnp.float32
    )
    for part in range(pooled_ref.shape[0] // LANES):
        out_ref[0, part : part + 1, :] = row[0:1, part * LANES : (part + 1) * LANES]


def partial_margins(pooled, step_dir):
    rows, cols = pooled.shape
    tile = tile_of(rows, 256)
    out = pl.pallas_call(
        margins_kernel,
        grid=(rows // tile,),
        in_specs=[
            pl.BlockSpec((8, cols), lambda i: (0, 0)),
            pl.BlockSpec((tile, cols), lambda i: (i, 0)),
        ],
        out_specs=pl.BlockSpec((1, tile // LANES, LANES), lambda i: (i, 0, 0)),
        out_shape=jax.ShapeDtypeStruct((rows // tile, tile // LANES, LANES), jnp.float32),
        compiler_params=PARAMS,
        cost_estimate=pl.CostEstimate(flops=2 * rows * cols, bytes_accessed=2 * rows * cols, transcendentals=0),
        name="margins",
    )(jnp.broadcast_to(step_dir[None, :], (8, cols)), pooled)
    return out.reshape(rows // LANES, LANES)


def fill_signs(signs_ref, sampled, ex_index, row_count):
    high_bits = row_count.bit_length() - 1
    lane = lax.broadcasted_iota(jnp.int32, sampled.shape, 1)
    folded = (sampled & lane) ^ (lax.shift_right_logical(sampled, high_bits) & ex_index)
    for shift_by in (16, 8, 4, 2, 1):
        folded = folded ^ lax.shift_right_logical(folded, shift_by)
    tiles = [(1 - 2 * (folded & 1)).astype(jnp.float32)]
    for bit in range(LANES.bit_length() - 1, high_bits):
        flip = (1 - 2 * (lax.shift_right_logical(sampled, bit) & 1)).astype(jnp.float32)
        tiles = tiles + [tile * flip for tile in tiles]
    for at, tile in enumerate(tiles):
        signs_ref[:, at * LANES : (at + 1) * LANES] = tile.astype(jnp.bfloat16)


def fill_scale(scale_col_ref, scale):
    groups = scale.shape[0]
    for at in range(groups):
        square = jnp.broadcast_to(scale[at : at + 1, :], (LANES, LANES))
        scale_col_ref[at * LANES : (at + 1) * LANES, :] = square.T


def weigh(pooled_ref, scale_col_ref):
    pieces = []
    for at in range(pooled_ref.shape[1] // LANES):
        part = pooled_ref[:, at * LANES : (at + 1) * LANES].astype(jnp.float32)
        pieces.append((part * scale_col_ref[...]).astype(jnp.bfloat16))
    return pieces[0] if len(pieces) == 1 else jnp.concatenate(pieces, axis=1)


def first_kernel(
    block_rows, ex_ref, mine_ref, theirs_ref, old_ref, labels_ref, bits_ref, sampled_ref, pooled_ref, *rest
):
    *outs, margins_ref, scale_ref, residual_ref, signs_ref, scale_col_ref = rest

    @pl.when(pl.program_id(0) == 0)
    def _():
        margins = old_ref[...] + (mine_ref[...] + theirs_ref[...])
        up, down = jax.nn.sigmoid(margins), jax.nn.sigmoid(-margins)
        scale = (2 * bits_ref[...] - 1).astype(jnp.float32) * jnp.sqrt(up * down)
        margins_ref[...] = margins
        scale_ref[...] = scale
        residual_ref[...] = up - labels_ref[...].astype(jnp.float32)
        fill_scale(scale_col_ref, scale)
        fill_signs(signs_ref, sampled_ref[...], ex_ref[0], pooled_ref.shape[0])

    weighted = weigh(pooled_ref, scale_col_ref)
    terms = jnp.dot(signs_ref[...], weighted, preferred_element_type=jnp.float32)
    for at, out in enumerate(outs):
        out[...] = terms[at * block_rows : (at + 1) * block_rows].astype(out.dtype)


def rest_kernel(block_rows, ex_ref, scale_ref, sampled_ref, pooled_ref, *rest):
    *outs, signs_ref, scale_col_ref = rest

    @pl.when(pl.program_id(0) == 0)
    def _():
        fill_scale(scale_col_ref, scale_ref[...])
        fill_signs(signs_ref, sampled_ref[...], ex_ref[0], pooled_ref.shape[0])

    weighted = weigh(pooled_ref, scale_col_ref)
    terms = jnp.dot(signs_ref[...], weighted, preferred_element_type=jnp.float32)
    for at, out in enumerate(outs):
        out[...] = terms[at * block_rows : (at + 1) * block_rows].astype(out.dtype)


def whole_spec(shape):
    return pl.BlockSpec(shape, lambda i: (0,) * len(shape))


def sketch_terms(kernel, name, ex_index, small, sampled, pooled, block_rows, kinds, extra=()):
    rows, cols = pooled.shape
    tile = tile_of(cols, 256)
    smem = pl.BlockSpec(memory_space=pltpu.SMEM)
    out_shape = [jax.ShapeDtypeStruct((block_rows, cols), kind) for kind in kinds]
    out_specs = [pl.BlockSpec((block_rows, tile), lambda i: (0, i)) for _ in kinds]
    out_shape += [jax.ShapeDtypeStruct(shape, jnp.float32) for shape in extra]
    out_specs += [whole_spec(shape) for shape in extra]
    return pl.pallas_call(
        functools.partial(kernel, block_rows),
        grid=(cols // tile,),
        in_specs=[smem]
        + [whole_spec(x.shape) for x in small]
        + [whole_spec(sampled.shape), pl.BlockSpec((rows, tile), lambda i: (0, i))],
        out_specs=out_specs,
        out_shape=out_shape,
        scratch_shapes=[
            pltpu.VMEM((sampled.shape[0], rows), jnp.bfloat16),
            pltpu.VMEM((rows, LANES), jnp.float32),
        ],
        compiler_params=PARAMS,
        cost_estimate=pl.CostEstimate(
            flops=2 * sampled.shape[0] * rows * cols, bytes_accessed=2 * rows * cols, transcendentals=0
        ),
        name=name,
    )(ex_index, *small, sampled, pooled)


def gradient_kernel(residual_ref, pooled_ref, out_ref):
    row = jnp.concatenate([residual_ref[at : at + 1, :] for at in range(residual_ref.shape[0])], axis=1)
    left = jnp.broadcast_to(row, (8, row.shape[1])).astype(jnp.bfloat16)
    out_ref[...] = jnp.dot(left, pooled_ref[...], preferred_element_type=jnp.float32)[0:1, :]


def gradient_terms(residual, pooled):
    rows, cols = pooled.shape
    tile = tile_of(cols, 256)
    return pl.pallas_call(
        gradient_kernel,
        grid=(cols // tile,),
        in_specs=[whole_spec(residual.shape), pl.BlockSpec((rows, tile), lambda i: (0, i))],
        out_specs=pl.BlockSpec((1, tile), lambda i: (0, i)),
        out_shape=jax.ShapeDtypeStruct((1, cols), jnp.float32),
        compiler_params=PARAMS,
        cost_estimate=pl.CostEstimate(flops=2 * rows * cols, bytes_accessed=2 * rows * cols, transcendentals=0),
        name="gradient",
    )(residual, pooled)


def flipped_by(value, index, bits):
    tail = value.shape[1:]
    cube = value.reshape((2,) * bits + tail)
    for bit in range(bits):
        axis = bits - 1 - bit
        cube = jnp.where((index >> bit) & 1 == 1, jnp.flip(cube, axis), cube)
    return cube.reshape((1 << bits,) + tail)


def on_device(pooled, labels, sign_bits, margins_old, direction, sample_rows):
    rows, cols = pooled.shape
    ex_count, feat_count = lax.axis_size("ex"), lax.axis_size("feat")
    bits = ex_count.bit_length() - 1
    ex_index = lax.axis_index("ex").astype(jnp.int32)
    total_rows = rows * ex_count
    sketch_count = sample_rows.shape[0]
    block_rows = sketch_count // ex_count
    dense = (rows // LANES, LANES)

    step_dir = direction.astype(jnp.bfloat16)
    for bit in range(bits):
        other = swap_with(step_dir, "ex", 1 << bit)
        low = (ex_index >> bit) & 1 == 0
        step_dir = jnp.concatenate([jnp.where(low, step_dir, other), jnp.where(low, other, step_dir)])

    terms = partial_margins(pooled, step_dir)
    distance = 1
    while distance < feat_count:
        mine, theirs = terms, swap_with(terms, "feat", distance)
        terms = mine + theirs
        distance *= 2

    order = send_order(bits)
    early = order[0][:2]
    late = [r for r in range(ex_count) if r not in early]
    leaving_at_once = set(order[0])
    by_owner = flipped_by(sample_rows.reshape(ex_count, block_rows), ex_index, bits)

    def sampled_of(blocks):
        picked = jnp.concatenate([by_owner[r] for r in blocks])
        return jnp.broadcast_to(picked[:, None], (picked.shape[0], LANES))

    def kinds_of(blocks):
        return [jnp.bfloat16 if r in leaving_at_once else jnp.float32 for r in blocks]

    ex_scalar = ex_index.reshape(1)
    *first, margins, scale, residual = sketch_terms(
        first_kernel,
        "first_terms",
        ex_scalar,
        [mine, theirs, margins_old.reshape(dense), labels.reshape(dense), sign_bits.reshape(dense)],
        sampled_of(early),
        pooled,
        block_rows,
        kinds_of(early),
        extra=[dense] * 3,
    )
    rest = sketch_terms(
        rest_kernel, "rest_terms", ex_scalar, [scale], sampled_of(late), pooled, block_rows, kinds_of(late)
    )
    held = dict(zip(early, first)) | dict(zip(late, rest))

    for bit, blocks in enumerate(order):
        for r in blocks:
            arrived = swap_with(held.pop(r).astype(jnp.bfloat16), "ex", 1 << bit)
            kept = r ^ (1 << bit)
            held[kept] = held[kept] + arrived.astype(jnp.float32)
    sketch = held[0] * (1 / math.sqrt(sketch_count))

    part = gradient_terms(residual, pooled)[0]
    for bit in reversed(range(bits)):
        low = (ex_index >> bit) & 1 == 0
        lower, upper = jnp.split(part, 2)
        arrived = swap_with(jnp.where(low, upper, lower), "ex", 1 << bit)
        part = jnp.where(low, lower, upper) + arrived
    gradient = part / math.sqrt(total_rows)
    return margins.reshape(rows), gradient, sketch


def solution(mesh):
    return jax.shard_map(
        on_device,
        mesh=mesh,
        in_specs=(P("ex", "feat"), P("ex"), P("ex"), P("ex"), P(("feat", "ex")), P()),
        out_specs=(P("ex"), P(("feat", "ex")), P("ex", "feat")),
        check_vma=False,
    )
```

time: 216 us -> 118 us (0.55)
  waiting for transfers between devices: 121 us -> 52.7 us
  blocking collectives: 46.7 us -> 0 us
  Pallas kernels: 0 us -> 35.1 us
  matrix products: 28.6 us -> 0 us
  starting transfers between devices: 0.04 us -> 22.9 us
  between operations: 14.8 us -> 0.81 us
    reduce_scatter x1 -> x0, waiting for transfers between devices: 121 us -> none  [on_device(): lax.psum_scatter(jnp.dot(signs_table, weighted, preferred_element_type=jn...]
    ppermute x0 -> x15, waiting for transfers between devices: none -> 52.7 us  [swap_with(): return lax.ppermute(value, axis, [(i, i ^ distance) for i in range(count)])]
    pallas_call x0 -> x4, Pallas kernels: none -> 35.1 us  [the longest x2 21.6 us: sketch_terms(): pl.pallas_call(functools.partial(kernel, block_rows), grid=(cols // tile,...]
    dot_general x3 -> x0, matrix products: 28.6 us -> none  [the longest x1 17.9 us: on_device(): jnp.dot(signs_table, weighted, preferred_element_type=jnp.float32)]
    ppermute x0 -> x15, starting transfers between devices: none -> 22.9 us  [swap_with(): return lax.ppermute(value, axis, [(i, i ^ distance) for i in range(count)])]
    all_gather x1 -> x0, blocking collectives: 22.2 us -> none  [on_device(): lax.all_gather(direction.astype(jnp.bfloat16), 'ex', axis=0, tiled=True)]
    unnamed x1 -> x0, blocking collectives: 18.7 us -> none
    psum x1 -> x0, blocking collectives: 5.75 us -> none  [on_device(): margins = margins_old + lax.psum(partial_margins, 'feat')]
  transfers between devices with their start and end apart: 1 -> 15, of which waited for: 1 -> 8; matrix products, arithmetic and copies ran while one was open for 3% -> 2% of each run, Pallas kernels for 0% -> 11%
where the time goes in v1:
time: 118 us; the launch traced here: 117 us
  waiting for transfers between devices  52.7 us (45%)
  Pallas kernels  35.1 us (30%)
  starting transfers between devices  22.9 us (19%)
  other arithmetic  4.45 us (4%)
    ppermute x15, waiting for transfers between devices, swap_with(): return lax.ppermute(value, axis, [(i, i ^ distance) for i in range(count)])  52.7 us
    ppermute x15, starting transfers between devices, swap_with(): return lax.ppermute(value, axis, [(i, i ^ distance) for i in range(count)])  22.9 us
    pallas_call x2, Pallas kernels, sketch_terms(): pl.pallas_call(functools.partial(kernel, block_rows), grid=(cols // tile,...  21.6 us
    pallas_call x1, Pallas kernels, partial_margins(): pl.pallas_call(margins_kernel, grid=(rows // tile,), in_specs=[pl.BlockSp...  7.06 us
    pallas_call x1, Pallas kernels, gradient_terms(): pl.pallas_call(gradient_kernel, grid=(cols // tile,), in_specs=[whole_spe...  6.47 us
  transfers between devices with their start and end apart: 15, of which 8 were waited for; matrix products, arithmetic and copies ran while one was open for 2% of the time, Pallas kernels for 11%

profile of v1, /device:TPU:0, one launch (start us, length us, event | category | flops | bytes accessed | tf_op | source)
XLA Modules:
  0.0 117.0 jit_solution(3069438252163602506)
XLA Ops:
  1.4 2.9 %collective-permute-start = (bf16[256]{0:T(256)(128)(2,1)S(1)}, bf16[256]{0:T(256)(128)(2,1)S(1)}, u32[]{:S(2)}, u32[]{:S(2)}) collective-permute-start(bf16[256]{0:T(256)(128)(2,1)S(1)} %convert_element_type.33), channel_id=1, source_target_pairs={{0,4},{4,0},{8,12},{12,8},{16,20},{20,16},{24,28},{28,24},{1,5},{5... | collective-permute-start | bytes 1544 | tf_op jit(solution)/shard_map/ppermute | solution.py:25
  4.3 0.7 rev.12
  6.5 2.2 %collective-permute-start.1 = (bf16[512]{0:T(512)(128)(2,1)S(1)}, bf16[512]{0:T(512)(128)(2,1)S(1)}, u32[]{:S(2)}, u32[]{:S(2)}) collective-permute-start(bf16[512]{0:T(512)(128)(2,1)S(1)} %pad_maximum_fusion.2), channel_id=1, source_target_pairs={{0,8},{4,12},{8,0},{12,4},{16,24},{20,28},{24,16},{28,20},{1,9},{5... | collective-permute-start | bytes 3080 | tf_op jit(solution)/shard_map/ppermute | solution.py:25
  8.7 1.5 %collective-permute-done.1 = bf16[512]{0:T(512)(128)(2,1)S(1)} collective-permute-done((bf16[512]{0:T(512)(128)(2,1)S(1)}, bf16[512]{0:T(512)(128)(2,1)S(1)}, u32[]{:S(2)}, u32[]{:S(2)}) %collective-permute-start.1) | collective-permute-done | bytes 1056 | tf_op jit(solution)/shard_map/ppermute | solution.py:25
  10.3 3.1 %collective-permute-start.2 = (bf16[1024]{0:T(1024)(128)(2,1)S(1)}, bf16[1024]{0:T(1024)(128)(2,1)S(1)}, u32[]{:S(2)}, u32[]{:S(2)}) collective-permute-start(bf16[1024]{0:T(1024)(128)(2,1)S(1)} %pad_maximum_fusion.1), channel_id=1, source_target_pairs={{0,16},{4,20},{8,24},{12,28},{16,0},{20,4},{24,8},{28,12},{1,17},{... | collective-permute-start | bytes 6152 | tf_op jit(solution)/shard_map/ppermute | solution.py:25
  13.4 1.6 %collective-permute-done.2 = bf16[1024]{0:T(1024)(128)(2,1)S(1)} collective-permute-done((bf16[1024]{0:T(1024)(128)(2,1)S(1)}, bf16[1024]{0:T(1024)(128)(2,1)S(1)}, u32[]{:S(2)}, u32[]{:S(2)}) %collective-permute-start.2) | collective-permute-done | bytes 2080 | tf_op jit(solution)/shard_map/ppermute | solution.py:25
  14.9 7.1 %margins.1 = f32[8,2,128]{2,1,0:T(2,128)S(1)} custom-call(bf16[8,2048]{1,0:T(8,128)(2,1)S(1)} %broadcast_in_dim.6.dir_ref, bf16[2048,2048]{1,0:T(8,128)(2,1)} %pooled_ref.7), custom_call_target="tpu_custom_call" | custom-call | flops 8388608 | bytes 8388608 | tf_op jit(solution)/shard_map/margins/pallas_call | solution.py:48
  22.0 1.2 collective-permute-done.3
  23.2 1.8 %collective-permute-start.4 = (f32[16,128]{1,0:T(8,128)S(1)}, f32[16,128]{1,0:T(8,128)S(1)}, u32[]{:S(2)}, u32[]{:S(2)}) collective-permute-start(f32[16,128]{1,0:T(8,128)S(1)} %add.33.mine_ref), channel_id=1, source_target_pairs={{0,2},{1,3},{2,0},{3,1},{4,6},{5,7},{6,4},{7,5},{8,10},{9,11},{10,... | collective-permute-start | bytes 24584 | tf_op jit(solution)/shard_map/ppermute | solution.py:25
  25.1 1.8 %collective-permute-done.4.theirs_ref = f32[16,128]{1,0:T(8,128)S(1)} collective-permute-done((f32[16,128]{1,0:T(8,128)S(1)}, f32[16,128]{1,0:T(8,128)S(1)}, u32[]{:S(2)}, u32[]{:S(2)}) %collective-permute-start.4) | collective-permute-done | bytes 8224 | tf_op jit(solution)/shard_map/ppermute | solution.py:25
  27.0 9.0 %first_terms.1 = (bf16[128,2048]{1,0:T(8,128)(2,1)S(1)}, bf16[128,2048]{1,0:T(8,128)(2,1)S(1)}, f32[16,128]{1,0:T(8,128)}, f32[16,128]{1,0:T(8,128)S(1)}, f32[16,128]{1,0:T(8,128)S(1)}) custom-call(s32[1]{0:T(128)} %bitcast.ex_ref, f32[16,128]{1,0:T(8,128)S(1)} %add.33.mine_ref, f32[16,128]{1,0:T(8,128)S(1)} %collective-permute-done.4.theirs_ref, ...), custom_call_target="tpu_custom_call" | custom-call | flops 2147483648 | bytes 8388608 | tf_op jit(solution)/shard_map/first_terms/pallas_call | solution.py:141
  35.9 6.5 %gradient.1 = f32[1,2048]{1,0:T(1,128)S(1)} custom-call(f32[16,128]{1,0:T(8,128)S(1)} %get-tuple-element.15.residual_ref, bf16[2048,2048]{1,0:T(8,128)(2,1)} %pooled_ref.7), custom_call_target="tpu_custom_call" | custom-call | flops 8388608 | bytes 8388608 | tf_op jit(solution)/shard_map/gradient/pallas_call | solution.py:170
  42.4 3.0 %collective-permute-start.5 = (f32[1024]{0:T(1024)S(1)}, f32[1024]{0:T(1024)S(1)}, u32[]{:S(2)}, u32[]{:S(2)}) collective-permute-start(f32[1024]{0:T(1024)S(1)} %bitcast.41), channel_id=1, source_target_pairs={{0,16},{4,20},{8,24},{12,28},{16,0},{20,4},{24,8},{28,12},{1,17},{... | collective-permute-start | bytes 12296 | tf_op jit(solution)/shard_map/ppermute | solution.py:25
  45.4 1.5 %collective-permute-start.9 = (bf16[128,2048]{1,0:T(8,128)(2,1)S(1)}, bf16[128,2048]{1,0:T(8,128)(2,1)S(1)}, u32[]{:S(2)}, u32[]{:S(2)}) collective-permute-start(bf16[128,2048]{1,0:T(8,128)(2,1)S(1)} %get-tuple-element.20), channel_id=1, source_target_pairs={{0,4},{4,0},{8,12},{12,8},{16,20},{20,16},{24,28},{28,24},{1,5},{5... | collective-permute-start | bytes 1572872 | tf_op jit(solution)/shard_map/ppermute | solution.py:25
  47.6 12.6 %rest_terms.1 = (f32[128,2048]{1,0:T(8,128)S(1)}, bf16[128,2048]{1,0:T(8,128)(2,1)S(1)}, f32[128,2048]{1,0:T(8,128)S(1)}, f32[128,2048]{1,0:T(8,128)S(1)}, bf16[...) custom-call(s32[1]{0:T(128)} %bitcast.ex_ref, f32[16,128]{1,0:T(8,128)S(1)} %get-tuple-element.16.scale_ref, ...), custom_call_target="tpu_custom_call" | custom-call | flops 6442450944 | bytes 8388608 | tf_op jit(solution)/shard_map/rest_terms/pallas_call | solution.py:141
  60.2 1.6 %collective-permute-start.8 = (bf16[128,2048]{1,0:T(8,128)(2,1)S(1)}, bf16[128,2048]{1,0:T(8,128)(2,1)S(1)}, u32[]{:S(2)}, u32[]{:S(2)}) collective-permute-start(bf16[128,2048]{1,0:T(8,128)(2,1)S(1)} %get-tuple-element.18), channel_id=1, source_target_pairs={{0,4},{4,0},{8,12},{12,8},{16,20},{20,16},{24,28},{28,24},{1,5},{5... | collective-permute-start | bytes 1572872 | tf_op jit(solution)/shard_map/ppermute | solution.py:25
  62.3 9.2 %collective-permute-done.12 = bf16[128,2048]{1,0:T(8,128)(2,1)S(1)} collective-permute-done((bf16[128,2048]{1,0:T(8,128)(2,1)S(1)}, bf16[128,2048]{1,0:T(8,128)(2,1)S(1)}, u32[]{:S(2)}, u32[]{:S(2)}) %collective-permute-start.12) | collective-permute-done | bytes 524320 | tf_op jit(solution)/shard_map/ppermute | solution.py:25
  71.6 1.7 %collective-permute-start.13 = (bf16[128,2048]{1,0:T(8,128)(2,1)S(1)}, bf16[128,2048]{1,0:T(8,128)(2,1)S(1)}, u32[]{:S(2)}, u32[]{:S(2)}) collective-permute-start(bf16[128,2048]{1,0:T(8,128)(2,1)S(1)} %add_convert_fusion.1), channel_id=1, source_target_pairs={{0,8},{4,12},{8,0},{12,4},{16,24},{20,28},{24,16},{28,20},{1,9},{5... | collective-permute-start | bytes 1572872 | tf_op jit(solution)/shard_map/ppermute | solution.py:25
  73.9 1.7 %collective-permute-start.10 = (bf16[128,2048]{1,0:T(8,128)(2,1)S(1)}, bf16[128,2048]{1,0:T(8,128)(2,1)S(1)}, u32[]{:S(2)}, u32[]{:S(2)}) collective-permute-start(bf16[128,2048]{1,0:T(8,128)(2,1)S(1)} %add_convert_fusion.2), channel_id=1, source_target_pairs={{0,8},{4,12},{8,0},{12,4},{16,24},{20,28},{24,16},{28,20},{1,9},{5... | collective-permute-start | bytes 1572872 | tf_op jit(solution)/shard_map/ppermute | solution.py:25
  75.5 16.2 %collective-permute-done.11 = bf16[128,2048]{1,0:T(8,128)(2,1)S(1)} collective-permute-done((bf16[128,2048]{1,0:T(8,128)(2,1)S(1)}, bf16[128,2048]{1,0:T(8,128)(2,1)S(1)}, u32[]{:S(2)}, u32[]{:S(2)}) %collective-permute-start.11) | collective-permute-done | bytes 524320 | tf_op jit(solution)/shard_map/ppermute | solution.py:25
  92.4 1.6 %collective-permute-start.7 = (f32[256]{0:T(256)S(1)}, f32[256]{0:T(256)S(1)}, u32[]{:S(2)}, u32[]{:S(2)}) collective-permute-start(f32[256]{0:T(256)S(1)} %broadcast_select_fusion.5), channel_id=1, source_target_pairs={{0,4},{4,0},{8,12},{12,8},{16,20},{20,16},{24,28},{28,24},{1,5},{5... | collective-permute-start | bytes 3080 | tf_op jit(solution)/shard_map/ppermute | solution.py:25
  93.9 2.1 %collective-permute-done.7 = f32[256]{0:T(256)S(1)} collective-permute-done((f32[256]{0:T(256)S(1)}, f32[256]{0:T(256)S(1)}, u32[]{:S(2)}, u32[]{:S(2)}) %collective-permute-start.7) | collective-permute-done | bytes 1056 | tf_op jit(solution)/shard_map/ppermute | solution.py:25
  96.6 19.2 %collective-permute-done.14 = bf16[128,2048]{1,0:T(8,128)(2,1)S(1)} collective-permute-done((bf16[128,2048]{1,0:T(8,128)(2,1)S(1)}, bf16[128,2048]{1,0:T(8,128)(2,1)S(1)}, u32[]{:S(2)}, u32[]{:S(2)}) %collective-permute-start.14) | collective-permute-done | bytes 524320 | tf_op jit(solution)/shard_map/ppermute | solution.py:25
  115.8 1.2 %add_multiply_fusion = f32[128,2048]{1,0:T(8,128)} fusion(bf16[128,2048]{1,0:T(8,128)(2,1)S(1)} %collective-permute-done.14, bf16[128,2048]{1,0:T(8,128)(2,1)S(1)} %collective-permute-done.10, f32[128,2048]{1,0:T(8,128)S(1)} %get-tuple-element.17, bf16[128,2048]{1,0:T(8,128)(2,1)S(1)} %collective-permute-done.8), kind=kLoop, calls=%fused_computation | loop fusion | flops 1835008 | bytes 3670016 | tf_op jit(solution)/shard_map/mul | solution.py:249
  (50 shorter events, 5.5 us)
Async XLA Ops:
  0.6 26.3 %copy-start = (f32[2048]{0:T(1024)S(1)}, f32[2048]{0:T(1024)}, u32[]{:S(2)}) copy-start(f32[2048]{0:T(1024)} %param.9) | copy-start | bytes 24580
  0.6 26.3 %copy-start.2 = (s32[2048]{0:T(1024)S(1)}, s32[2048]{0:T(1024)}, u32[]{:S(2)}) copy-start(s32[2048]{0:T(1024)} %param.8) | copy-start | bytes 24580
  0.7 26.3 %copy-start.1 = (s32[2048]{0:T(1024)S(1)}, s32[2048]{0:T(1024)}, u32[]{:S(2)}) copy-start(s32[2048]{0:T(1024)} %param.7) | copy-start | bytes 24580
  1.4 4.5 %collective-permute-start = (bf16[256]{0:T(256)(128)(2,1)S(1)}, bf16[256]{0:T(256)(128)(2,1)S(1)}, u32[]{:S(2)}, u32[]{:S(2)}) collective-permute-start(bf16[256]{0:T(256)(128)(2,1)S(1)} %convert_element_type.33), channel_id=1, source_target_pairs={{0,4},{4,0},{8,12},{12,8},{16,20},{20,16},{24,28},{28,24},{1,5},{5... | collective-permute-start | bytes 1544 | tf_op jit(solution)/shard_map/ppermute | solution.py:25
  6.5 3.7 %collective-permute-start.1 = (bf16[512]{0:T(512)(128)(2,1)S(1)}, bf16[512]{0:T(512)(128)(2,1)S(1)}, u32[]{:S(2)}, u32[]{:S(2)}) collective-permute-start(bf16[512]{0:T(512)(128)(2,1)S(1)} %pad_maximum_fusion.2), channel_id=1, source_target_pairs={{0,8},{4,12},{8,0},{12,4},{16,24},{20,28},{24,16},{28,20},{1,9},{5... | collective-permute-start | bytes 3080 | tf_op jit(solution)/shard_map/ppermute | solution.py:25
  10.3 4.7 %collective-permute-start.2 = (bf16[1024]{0:T(1024)(128)(2,1)S(1)}, bf16[1024]{0:T(1024)(128)(2,1)S(1)}, u32[]{:S(2)}, u32[]{:S(2)}) collective-permute-start(bf16[1024]{0:T(1024)(128)(2,1)S(1)} %pad_maximum_fusion.1), channel_id=1, source_target_pairs={{0,16},{4,20},{8,24},{12,28},{16,0},{20,4},{24,8},{28,12},{1,17},{... | collective-permute-start | bytes 6152 | tf_op jit(solution)/shard_map/ppermute | solution.py:25
  22.0 1.2 %collective-permute-start.3 = (f32[16,128]{1,0:T(8,128)S(1)}, f32[16,128]{1,0:T(8,128)S(1)}, u32[]{:S(2)}, u32[]{:S(2)}) collective-permute-start(f32[16,128]{1,0:T(8,128)S(1)} %bitcast.26), channel_id=1, source_target_pairs={{0,1},{1,0},{2,3},{3,2},{4,5},{5,4},{6,7},{7,6},{8,9},{9,8},{10,11... | collective-permute-start | bytes 24584 | tf_op jit(solution)/shard_map/ppermute | solution.py:25
  23.2 3.7 %collective-permute-start.4 = (f32[16,128]{1,0:T(8,128)S(1)}, f32[16,128]{1,0:T(8,128)S(1)}, u32[]{:S(2)}, u32[]{:S(2)}) collective-permute-start(f32[16,128]{1,0:T(8,128)S(1)} %add.33.mine_ref), channel_id=1, source_target_pairs={{0,2},{1,3},{2,0},{3,1},{4,6},{5,7},{6,4},{7,5},{8,10},{9,11},{10,... | collective-permute-start | bytes 24584 | tf_op jit(solution)/shard_map/ppermute | solution.py:25
  42.4 19.9 %collective-permute-start.5 = (f32[1024]{0:T(1024)S(1)}, f32[1024]{0:T(1024)S(1)}, u32[]{:S(2)}, u32[]{:S(2)}) collective-permute-start(f32[1024]{0:T(1024)S(1)} %bitcast.41), channel_id=1, source_target_pairs={{0,16},{4,20},{8,24},{12,28},{16,0},{20,4},{24,8},{28,12},{1,17},{... | collective-permute-start | bytes 12296 | tf_op jit(solution)/shard_map/ppermute | solution.py:25
  45.4 28.3 %collective-permute-start.9 = (bf16[128,2048]{1,0:T(8,128)(2,1)S(1)}, bf16[128,2048]{1,0:T(8,128)(2,1)S(1)}, u32[]{:S(2)}, u32[]{:S(2)}) collective-permute-start(bf16[128,2048]{1,0:T(8,128)(2,1)S(1)} %get-tuple-element.20), channel_id=1, source_target_pairs={{0,4},{4,0},{8,12},{12,8},{16,20},{20,16},{24,28},{28,24},{1,5},{5... | collective-permute-start | bytes 1572872 | tf_op jit(solution)/shard_map/ppermute | solution.py:25
  46.9 24.6 %collective-permute-start.12 = (bf16[128,2048]{1,0:T(8,128)(2,1)S(1)}, bf16[128,2048]{1,0:T(8,128)(2,1)S(1)}, u32[]{:S(2)}, u32[]{:S(2)}) collective-permute-start(bf16[128,2048]{1,0:T(8,128)(2,1)S(1)} %get-tuple-element.24), channel_id=1, source_target_pairs={{0,4},{4,0},{8,12},{12,8},{16,20},{20,16},{24,28},{28,24},{1,5},{5... | collective-permute-start | bytes 1572872 | tf_op jit(solution)/shard_map/ppermute | solution.py:25
  60.2 36.3 %collective-permute-start.8 = (bf16[128,2048]{1,0:T(8,128)(2,1)S(1)}, bf16[128,2048]{1,0:T(8,128)(2,1)S(1)}, u32[]{:S(2)}, u32[]{:S(2)}) collective-permute-start(bf16[128,2048]{1,0:T(8,128)(2,1)S(1)} %get-tuple-element.18), channel_id=1, source_target_pairs={{0,4},{4,0},{8,12},{12,8},{16,20},{20,16},{24,28},{28,24},{1,5},{5... | collective-permute-start | bytes 1572872 | tf_op jit(solution)/shard_map/ppermute | solution.py:25
  61.8 29.9 %collective-permute-start.11 = (bf16[128,2048]{1,0:T(8,128)(2,1)S(1)}, bf16[128,2048]{1,0:T(8,128)(2,1)S(1)}, u32[]{:S(2)}, u32[]{:S(2)}) collective-permute-start(bf16[128,2048]{1,0:T(8,128)(2,1)S(1)} %get-tuple-element.22), channel_id=1, source_target_pairs={{0,4},{4,0},{8,12},{12,8},{16,20},{20,16},{24,28},{28,24},{1,5},{5... | collective-permute-start | bytes 1572872 | tf_op jit(solution)/shard_map/ppermute | solution.py:25
  71.6 20.1 %collective-permute-start.13 = (bf16[128,2048]{1,0:T(8,128)(2,1)S(1)}, bf16[128,2048]{1,0:T(8,128)(2,1)S(1)}, u32[]{:S(2)}, u32[]{:S(2)}) collective-permute-start(bf16[128,2048]{1,0:T(8,128)(2,1)S(1)} %add_convert_fusion.1), channel_id=1, source_target_pairs={{0,8},{4,12},{8,0},{12,4},{16,24},{20,28},{24,16},{28,20},{1,9},{5... | collective-permute-start | bytes 1572872 | tf_op jit(solution)/shard_map/ppermute | solution.py:25
  73.3 19.0 %collective-permute-start.6 = (f32[512]{0:T(512)S(1)}, f32[512]{0:T(512)S(1)}, u32[]{:S(2)}, u32[]{:S(2)}) collective-permute-start(f32[512]{0:T(512)S(1)} %slice_select_fusion), channel_id=1, source_target_pairs={{0,8},{4,12},{8,0},{12,4},{16,24},{20,28},{24,16},{28,20},{1,9},{5... | collective-permute-start | bytes 6152 | tf_op jit(solution)/shard_map/ppermute | solution.py:25
  73.9 22.7 %collective-permute-start.10 = (bf16[128,2048]{1,0:T(8,128)(2,1)S(1)}, bf16[128,2048]{1,0:T(8,128)(2,1)S(1)}, u32[]{:S(2)}, u32[]{:S(2)}) collective-permute-start(bf16[128,2048]{1,0:T(8,128)(2,1)S(1)} %add_convert_fusion.2), channel_id=1, source_target_pairs={{0,8},{4,12},{8,0},{12,4},{16,24},{20,28},{24,16},{28,20},{1,9},{5... | collective-permute-start | bytes 1572872 | tf_op jit(solution)/shard_map/ppermute | solution.py:25
  91.9 23.9 %collective-permute-start.14 = (bf16[128,2048]{1,0:T(8,128)(2,1)S(1)}, bf16[128,2048]{1,0:T(8,128)(2,1)S(1)}, u32[]{:S(2)}, u32[]{:S(2)}) collective-permute-start(bf16[128,2048]{1,0:T(8,128)(2,1)S(1)} %add_convert_fusion), channel_id=1, source_target_pairs={{0,16},{4,20},{8,24},{12,28},{16,0},{20,4},{24,8},{28,12},{1,17},{... | collective-permute-start | bytes 1572872 | tf_op jit(solution)/shard_map/ppermute | solution.py:25
  92.4 3.6 %collective-permute-start.7 = (f32[256]{0:T(256)S(1)}, f32[256]{0:T(256)S(1)}, u32[]{:S(2)}, u32[]{:S(2)}) collective-permute-start(f32[256]{0:T(256)S(1)} %broadcast_select_fusion.5), channel_id=1, source_target_pairs={{0,4},{4,0},{8,12},{12,8},{16,20},{20,16},{24,28},{28,24},{1,5},{5... | collective-permute-start | bytes 3080 | tf_op jit(solution)/shard_map/ppermute | solution.py:25

commit v2 on v0

v2 whole, which is shorter than its diff:
```python
import functools
import math

import jax
import jax.numpy as jnp
from jax import lax
from jax.experimental import pallas as pl
from jax.experimental.pallas import tpu as pltpu
from jax.sharding import PartitionSpec as P

LANES = 128
VMEM_LIMIT = 40 * 1024 * 1024
PARAMS = pltpu.CompilerParams(vmem_limit_bytes=VMEM_LIMIT)


def tile_of(extent, most):
    size = most
    while extent % size:
        size //= 2
    return size


def swap_with(value, axis, distance):
    count = lax.axis_size(axis)
    return lax.ppermute(value, axis, [(i, i ^ distance) for i in range(count)])


def call_in_vmem(kernel, name, out_shape, scratch, flops, *operands, scalars=()):
    vmem, smem = pl.BlockSpec(memory_space=pltpu.VMEM), pl.BlockSpec(memory_space=pltpu.SMEM)
    return pl.pallas_call(
        kernel,
        in_specs=[smem] * len(scalars) + [vmem] * len(operands),
        out_specs=[vmem] * len(out_shape),
        out_shape=[jax.ShapeDtypeStruct(*entry) for entry in out_shape],
        scratch_shapes=scratch,
        compiler_params=PARAMS,
        cost_estimate=pl.CostEstimate(flops=0, bytes_accessed=0, transcendentals=0),
        name=name,
    )(*scalars, *(x if x.size < 1 << 18 else pltpu.with_memory_space_constraint(x, pltpu.VMEM) for x in operands))


def margins_kernel(dir_ref, pooled_ref, out_ref):
    rows = pooled_ref.shape[0]
    tile = tile_of(rows, 512)
    for at in range(0, rows, tile):
        row = lax.dot_general(
            dir_ref[...],
            pooled_ref[at : at + tile, :],
            (((1,), (1,)), ((), ())),
            preferred_element_type=jnp.float32,
        )
        for part in range(0, tile, LANES):
            group = (at + part) // LANES
            out_ref[group : group + 1, :] = row[0:1, part : part + LANES]


def fill_signs(signs_ref, sampled, ex_index):
    high_bits = signs_ref.shape[1].bit_length() - 1
    lane = lax.broadcasted_iota(jnp.int32, sampled.shape, 1)
    folded = (sampled & lane) ^ (lax.shift_right_logical(sampled, high_bits) & ex_index)
    for shift_by in (16, 8, 4, 2, 1):
        folded = folded ^ lax.shift_right_logical(folded, shift_by)
    tiles = [(1 - 2 * (folded & 1)).astype(jnp.float32)]
    for bit in range(LANES.bit_length() - 1, high_bits):
        flip = (1 - 2 * (lax.shift_right_logical(sampled, bit) & 1)).astype(jnp.float32)
        tiles = tiles + [tile * flip for tile in tiles]
    for at, tile in enumerate(tiles):
        signs_ref[:, at * LANES : (at + 1) * LANES] = tile.astype(jnp.bfloat16)


def fill_scale(scale_col_ref, scale):
    for at in range(scale.shape[0]):
        square = jnp.broadcast_to(scale[at : at + 1, :], (LANES, LANES))
        scale_col_ref[at * LANES : (at + 1) * LANES, :] = square.T


def weigh(pooled, scale_col):
    pieces = []
    for at in range(0, pooled.shape[1], LANES):
        part = pooled[:, at : at + LANES].astype(jnp.float32)
        pieces.append((part * scale_col).astype(jnp.bfloat16))
    return pieces[0] if len(pieces) == 1 else jnp.concatenate(pieces, axis=1)


def write_terms(cols, block_rows, pooled_ref, signs_ref, scale_col_ref, outs):
    tile = tile_of(cols, 256)
    for at in range(0, cols, tile):
        weighted = weigh(pooled_ref[:, at : at + tile], scale_col_ref[...])
        terms = jnp.dot(signs_ref[...], weighted, preferred_element_type=jnp.float32)
        for k, out in enumerate(outs):
            out[:, at : at + tile] = terms[k * block_rows : (k + 1) * block_rows].astype(out.dtype)


def first_kernel(
    cols, block_rows, ex_ref, mine_ref, theirs_ref, old_ref, labels_ref, bits_ref, sampled_ref, pooled_ref, *rest
):
    *outs, margins_ref, scale_ref, residual_ref, signs_ref, scale_col_ref = rest
    margins = old_ref[...] + (mine_ref[...] + theirs_ref[...])
    up, down = jax.nn.sigmoid(margins), jax.nn.sigmoid(-margins)
    scale = (2 * bits_ref[...] - 1).astype(jnp.float32) * jnp.sqrt(up * down)
    margins_ref[...] = margins
    scale_ref[...] = scale
    residual_ref[...] = up - labels_ref[...].astype(jnp.float32)
    fill_scale(scale_col_ref, scale)
    fill_signs(signs_ref, sampled_ref[...], ex_ref[0])
    write_terms(cols, block_rows, pooled_ref, signs_ref, scale_col_ref, outs)


def more_kernel(cols, block_rows, ex_ref, scale_ref, sampled_ref, pooled_ref, *rest):
    *outs, signs_ref, scale_col_ref = rest
    fill_scale(scale_col_ref, scale_ref[...])
    fill_signs(signs_ref, sampled_ref[...], ex_ref[0])
    write_terms(cols, block_rows, pooled_ref, signs_ref, scale_col_ref, outs)


def terms_of(kernel, name, cols, block_rows, ex_scalar, small, sampled, pooled, kinds, extra=()):
    rows = pooled.shape[0]
    return call_in_vmem(
        functools.partial(kernel, cols, block_rows),
        name,
        [((block_rows, cols), kind) for kind in kinds] + [(shape, jnp.float32) for shape in extra],
        [pltpu.VMEM((sampled.shape[0], rows), jnp.bfloat16), pltpu.VMEM((rows, LANES), jnp.float32)],
        2 * sampled.shape[0] * rows * cols,
        *small,
        sampled,
        pooled,
        scalars=(ex_scalar,),
    )


def pair_kernel(first_col, ex_ref, scale_ref, scale2_ref, sampled_ref, pooled_ref, theirs_ref, *rest):
    *outs, signs_ref, scale_col_ref = rest
    half = theirs_ref.shape[1]
    high_bits = signs_ref.shape[1].bit_length() - 1
    fill_signs(signs_ref, sampled_ref[...], ex_ref[0])
    flip = (1 - 2 * (lax.shift_right_logical(sampled_ref[...], high_bits) & 1)).astype(jnp.float32)
    start = pl.multiple_of(first_col + (ex_ref[0] & 1) * half, LANES)
    fill_scale(scale_col_ref, scale_ref[...])
    own = jnp.dot(
        signs_ref[...],
        weigh(pooled_ref[:, pl.ds(start, half)], scale_col_ref[...]),
        preferred_element_type=jnp.float32,
    )
    fill_scale(scale_col_ref, scale2_ref[...])
    other = jnp.dot(
        signs_ref[...], weigh(theirs_ref[...], scale_col_ref[...]), preferred_element_type=jnp.float32
    )
    for at in range(0, half, LANES):
        terms = own[:, at : at + LANES] + flip * other[:, at : at + LANES]
        row = 0
        for out in outs:
            out[:, at : at + LANES] = terms[row : row + out.shape[0]].astype(out.dtype)
            row += out.shape[0]


def gradient_kernel(residual_ref, pooled_ref, out_ref):
    row = jnp.concatenate([residual_ref[at : at + 1, :] for at in range(residual_ref.shape[0])], axis=1)
    left = jnp.broadcast_to(row, (8, row.shape[1])).astype(jnp.bfloat16)
    tile = tile_of(pooled_ref.shape[1], 512)
    for at in range(0, pooled_ref.shape[1], tile):
        terms = jnp.dot(left, pooled_ref[:, at : at + tile], preferred_element_type=jnp.float32)
        out_ref[:, at : at + tile] = terms[0:1, :]


def flipped_by(value, index, bits):
    tail = value.shape[1:]
    cube = value.reshape((2,) * bits + tail)
    for bit in range(bits):
        axis = bits - 1 - bit
        cube = jnp.where((index >> bit) & 1 == 1, jnp.flip(cube, axis), cube)
    return cube.reshape((1 << bits,) + tail)


def after(value, *others):
    return lax.optimization_barrier((value, *others))[0]


def wide(value):
    return value.astype(jnp.float32)


def on_device(pooled, labels, sign_bits, margins_old, direction, sample_rows):
    rows, cols = pooled.shape
    ex_count, feat_count = lax.axis_size("ex"), lax.axis_size("feat")
    bits = ex_count.bit_length() - 1
    ex_index = lax.axis_index("ex").astype(jnp.int32)
    total_rows = rows * ex_count
    sketch_count = sample_rows.shape[0]
    block_rows = sketch_count // ex_count
    dense = (rows // LANES, LANES)
    half = cols // 8 if cols % (8 * LANES) == 0 and bits > 1 else 0
    plain = cols - 2 * half
    odd = ex_index & 1 == 1

    step_dir = direction
    raw = None
    for bit in range(bits):
        other = swap_with(step_dir.astype(jnp.bfloat16), "ex", 1 << bit)
        low = (ex_index >> bit) & 1 == 0
        own = step_dir.astype(jnp.bfloat16)
        step_dir = jnp.concatenate([jnp.where(low, own, other), jnp.where(low, other, own)])
        if half and raw is None:
            leaving = jnp.where(odd, pooled[:, plain : plain + half], pooled[:, plain + half :])
            raw = swap_with(after(leaving, other), "ex", 1)

    (terms,) = call_in_vmem(
        margins_kernel,
        "margins",
        [(dense, jnp.float32)],
        [],
        2 * rows * cols,
        jnp.broadcast_to(step_dir[None, :], (8, cols)),
        pooled,
    )
    mine, theirs = terms, jnp.zeros_like(terms)
    distance = 1
    while distance < feat_count:
        mine = terms
        theirs = swap_with(mine, "feat", distance)
        terms = mine + theirs
        distance *= 2

    by_owner = flipped_by(sample_rows.reshape(ex_count, block_rows), ex_index, bits)
    order = [[r for r in range(ex_count - 1, 0, -1) if r & ((2 << bit) - 1) == 1 << bit] for bit in range(bits)]
    first = order[0][:1]
    second = order[0][1:2] + [order[0][0] ^ 1]
    third = [r for r in range(ex_count) if r not in first + second]

    def sampled_of(blocks):
        picked = jnp.concatenate([by_owner[r] for r in blocks])
        return jnp.broadcast_to(picked[:, None], (picked.shape[0], LANES))

    def kinds_of(blocks):
        return [jnp.bfloat16 if r & 1 else jnp.float32 for r in blocks]

    ex_scalar = ex_index.reshape(1)
    *made, margins, scale, residual = terms_of(
        first_kernel,
        "first_terms",
        plain,
        block_rows,
        ex_scalar,
        [mine, theirs, margins_old.reshape(dense), labels.reshape(dense), sign_bits.reshape(dense)],
        sampled_of(first),
        pooled,
        kinds_of(first),
        extra=[dense] * 3,
    )
    held = dict(zip(first, made))
    if half:
        scale_theirs = swap_with(scale, "ex", 1)

    def more(blocks, name, scale):
        if blocks:
            made = terms_of(
                more_kernel, name, plain, block_rows, ex_scalar, [scale], sampled_of(blocks), pooled, kinds_of(blocks)
            )
            held.update(zip(blocks, made))

    more(second, "second_terms", after(scale, raw) if half else scale)

    if half:
        groups, left = [], sorted(range(ex_count), key=lambda r: [r >> b & 1 for b in (*range(1, bits), 0)])
        for bit in range(1, bits):
            groups.append([r for r in left if r >> bit & 1])
            left = [r for r in left if not r >> bit & 1]
        groups += [[1], [0]]
        pair = call_in_vmem(
            functools.partial(pair_kernel, plain),
            "pair_terms",
            [
                ((len(group) * block_rows, half), jnp.bfloat16 if at == 0 else jnp.float32)
                for at, group in enumerate(groups)
            ],
            [pltpu.VMEM((sketch_count, rows), jnp.bfloat16), pltpu.VMEM((rows, LANES), jnp.float32)],
            4 * sketch_count * rows * half,
            after(scale, *held.values()),
            scale_theirs,
            sampled_of([r for group in groups for r in group]),
            pooled,
            raw,
            scalars=(ex_scalar,),
        )
        pair = [wide(x) for x in pair]
        for at in range(bits - 1):
            arrived = wide(swap_with(pair[at].astype(jnp.bfloat16), "ex", 2 << at))
            row = 0
            for later in range(bits, at, -1):
                size = pair[later].shape[0]
                pair[later] = pair[later] + arrived[row : row + size]
                row += size
        moved = wide(swap_with(pair[-2].astype(jnp.bfloat16), "ex", 1))

    def exchange(r):
        bit = (r & -r).bit_length() - 1
        arrived = wide(swap_with(held.pop(r).astype(jnp.bfloat16), "ex", 1 << bit))
        held[r ^ (1 << bit)] = held[r ^ (1 << bit)] + arrived

    exchange(order[0][0])
    more(third, "third_terms", after(scale, held[order[0][0] ^ 1]))
    held_late = [held[0]]
    for bit, blocks in enumerate(order):
        for r in blocks:
            if r in held:
                exchange(r)
            if bit == bits - 2 and r == blocks[0]:
                held_late = [held[r ^ (1 << bit)]]
    sketch = held[0]
    if half:
        sketch = jnp.concatenate(
            [sketch, jnp.where(odd, moved, pair[-1]), jnp.where(odd, pair[-1], moved)], axis=1
        )
    sketch = sketch * (1 / math.sqrt(sketch_count))

    (part,) = call_in_vmem(
        gradient_kernel,
        "gradient",
        [((1, cols), jnp.float32)],
        [],
        2 * rows * cols,
        after(residual, *held_late),
        pooled,
    )
    part = part[0]
    for bit in reversed(range(bits)):
        low = (ex_index >> bit) & 1 == 0
        lower, upper = jnp.split(part, 2)
        arrived = swap_with(jnp.where(low, upper, lower), "ex", 1 << bit)
        part = jnp.where(low, lower, upper) + arrived
    gradient = part / math.sqrt(total_rows)
    return margins.reshape(rows), gradient, sketch


def solution(mesh):
    return jax.shard_map(
        on_device,
        mesh=mesh,
        in_specs=(P("ex", "feat"), P("ex"), P("ex"), P("ex"), P(("feat", "ex")), P()),
        out_specs=(P("ex"), P(("feat", "ex")), P("ex", "feat")),
        check_vma=False,
    )
```

time: 216 us -> 94.3 us (0.44)
  waiting for transfers between devices: 121 us -> 45.6 us
  blocking collectives: 46.7 us -> 0 us
  matrix products: 28.6 us -> 0 us
  starting transfers between devices: 0.04 us -> 21.3 us
  Pallas kernels: 0 us -> 15.4 us
  between operations: 14.8 us -> 0.88 us
  local copies, waits for them, and re-layouts: 1.28 us -> 4.66 us
  other arithmetic: 3.65 us -> 6.14 us
    reduce_scatter x1 -> x0, waiting for transfers between devices: 121 us -> none  [on_device(): lax.psum_scatter(jnp.dot(signs_table, weighted, preferred_element_type=jn...]
    ppermute x0 -> x20, waiting for transfers between devices: none -> 45.6 us  [swap_with(): return lax.ppermute(value, axis, [(i, i ^ distance) for i in range(count)])]
    dot_general x3 -> x0, matrix products: 28.6 us -> none  [the longest x1 17.9 us: on_device(): jnp.dot(signs_table, weighted, preferred_element_type=jnp.float32)]
    all_gather x1 -> x0, blocking collectives: 22.2 us -> none  [on_device(): lax.all_gather(direction.astype(jnp.bfloat16), 'ex', axis=0, tiled=True)]
    ppermute x0 -> x20, starting transfers between devices: none -> 21.3 us  [swap_with(): return lax.ppermute(value, axis, [(i, i ^ distance) for i in range(count)])]
    unnamed x1 -> x0, blocking collectives: 18.7 us -> none
    pallas_call x0 -> x6, Pallas kernels: none -> 15.4 us  [call_in_vmem(): pl.pallas_call(kernel, in_specs=[smem] * len(scalars) + [vmem] * len(oper...]
    psum x1 -> x0, blocking collectives: 5.75 us -> none  [on_device(): margins = margins_old + lax.psum(partial_margins, 'feat')]
  transfers between devices with their start and end apart: 1 -> 20, of which waited for: 1 -> 12; matrix products, arithmetic and copies ran while one was open for 3% -> 5% of each run, Pallas kernels for 0% -> 16%
where the time goes in v2:
time: 94.3 us; the launch traced here: 94 us
  waiting for transfers between devices  45.6 us (48%)
  starting transfers between devices  21.3 us (23%)
  Pallas kernels  15.4 us (16%)
  other arithmetic  6.14 us (7%)
  local copies, waits for them, and re-layouts  4.66 us (5%)
    ppermute x20, waiting for transfers between devices, swap_with(): return lax.ppermute(value, axis, [(i, i ^ distance) for i in range(count)])  45.6 us
    ppermute x20, starting transfers between devices, swap_with(): return lax.ppermute(value, axis, [(i, i ^ distance) for i in range(count)])  21.3 us
    pallas_call x6, Pallas kernels, call_in_vmem(): pl.pallas_call(kernel, in_specs=[smem] * len(scalars) + [vmem] * len(oper...  15.4 us
    unnamed x15, local copies, waits for them, and re-layouts  3.44 us
  transfers between devices with their start and end apart: 20, of which 12 were waited for; matrix products, arithmetic and copies ran while one was open for 5% of the time, Pallas kernels for 16%

profile of v2, /device:TPU:0, one launch (start us, length us, event | category | flops | bytes accessed | tf_op | source)
XLA Modules:
  0.0 94.0 jit_solution(16482577025715245195)
XLA Ops:
  1.4 2.9 %collective-permute-start = (bf16[256]{0:T(256)(128)(2,1)S(1)}, bf16[256]{0:T(256)(128)(2,1)S(1)}, u32[]{:S(2)}, u32[]{:S(2)}) collective-permute-start(bf16[256]{0:T(256)(128)(2,1)S(1)} %convert_element_type.51), channel_id=1, source_target_pairs={{0,4},{4,0},{8,12},{12,8},{16,20},{20,16},{24,28},{28,24},{1,5},{5... | collective-permute-start | bytes 1544 | tf_op jit(solution)/shard_map/ppermute | solution.py:25
  5.7 1.7 %slice_select_fusion = bf16[2048,256]{1,0:T(8,128)(2,1)S(1)} fusion(bf16[2048,2048]{1,0:T(8,128)(2,1)} %pooled_ref.11, pred[]{:T(512)S(6)} %eq.30), kind=kLoop, calls=%fused_computation.1 | loop fusion | flops 524288 | bytes 3145729 | tf_op jit(solution)/shard_map/jit(_where)/select_n | solution.py:203
  9.8 2.0 %collective-permute-done.1 = bf16[512]{0:T(512)(128)(2,1)S(1)} collective-permute-done((bf16[512]{0:T(512)(128)(2,1)S(1)}, bf16[512]{0:T(512)(128)(2,1)S(1)}, u32[]{:S(2)}, u32[]{:S(2)}) %collective-permute-start.1) | collective-permute-done | bytes 1056 | tf_op jit(solution)/shard_map/ppermute | solution.py:25
  11.8 2.7 %collective-permute-start.2 = (bf16[1024]{0:T(1024)(128)(2,1)S(1)}, bf16[1024]{0:T(1024)(128)(2,1)S(1)}, u32[]{:S(2)}, u32[]{:S(2)}) collective-permute-start(bf16[1024]{0:T(1024)(128)(2,1)S(1)} %pad_maximum_fusion.1), channel_id=1, source_target_pairs={{0,16},{4,20},{8,24},{12,28},{16,0},{20,4},{24,8},{28,12},{1,17},{... | collective-permute-start | bytes 6152 | tf_op jit(solution)/shard_map/ppermute | solution.py:25
  16.4 3.4 %copy-done = bf16[2048,2048]{1,0:T(8,128)(2,1)S(1)} copy-done((bf16[2048,2048]{1,0:T(8,128)(2,1)S(1)}, bf16[2048,2048]{1,0:T(8,128)(2,1)}, u32[]{:S(2)}) %copy-start) | copy-done | bytes 8388632
  19.8 2.3 %margins.1 = f32[16,128]{1,0:T(8,128)S(1)} custom-call(bf16[8,2048]{1,0:T(8,128)(2,1)S(1)} %broadcast_in_dim.12.dir_ref, bf16[2048,2048]{1,0:T(8,128)(2,1)S(1)} %copy-done), custom_call_target="tpu_custom_call" | custom-call | tf_op jit(solution)/shard_map/margins/pallas_call | solution.py:30
  24.7 2.1 %collective-permute-done.4.theirs_ref = f32[16,128]{1,0:T(8,128)S(1)} collective-permute-done((f32[16,128]{1,0:T(8,128)S(1)}, f32[16,128]{1,0:T(8,128)S(1)}, u32[]{:S(2)}, u32[]{:S(2)}) %collective-permute-start.4) | collective-permute-done | bytes 8224 | tf_op jit(solution)/shard_map/ppermute | solution.py:25
  27.0 2.0 %first_terms.1 = (bf16[128,1536]{1,0:T(8,128)(2,1)S(1)}, f32[16,128]{1,0:T(8,128)}, f32[16,128]{1,0:T(8,128)S(1)}, f32[16,128]{1,0:T(8,128)S(1)}) custom-call(s32[1]{0:T(128)} %bitcast.ex_ref, f32[16,128]{1,0:T(8,128)S(1)} %add.48.mine_ref, f32[16,128]{1,0:T(8,128)S(1)} %collective-permute-done.4.theirs_ref, f32[16,128]{1,0:T(8,128)S(1)} %bitcast.36, ...), custom_call_target="tpu_custom_call" | custom-call | tf_op jit(solution)/shard_map/first_terms/pallas_call | solution.py:30
  29.4 1.7 %collective-permute-start.16 = (f32[16,128]{1,0:T(8,128)S(1)}, f32[16,128]{1,0:T(8,128)S(1)}, u32[]{:S(2)}, u32[]{:S(2)}) collective-permute-start(f32[16,128]{1,0:T(8,128)S(1)} %get-tuple-element.38.scale_ref), channel_id=1, source_target_pairs={{0,4},{4,0},{8,12},{12,8},{16,20},{20,16},{24,28},{28,24},{1,5},{5... | collective-permute-start | bytes 24584 | tf_op jit(solution)/shard_map/ppermute | solution.py:25
  31.1 9.4 %collective-permute-done.5.theirs_ref = bf16[2048,256]{1,0:T(8,128)(2,1)S(1)} collective-permute-done((bf16[2048,256]{1,0:T(8,128)(2,1)S(1)}, bf16[2048,256]{1,0:T(8,128)(2,1)S(1)}, u32[]{:S(2)}, u32[]{:S(2)}) %collective-permute-start.5) | collective-permute-done | bytes 1048608 | tf_op jit(solution)/shard_map/ppermute | solution.py:25
  40.7 2.2 %second_terms.1 = (bf16[128,1536]{1,0:T(8,128)(2,1)S(1)}, f32[128,1536]{1,0:T(8,128)S(1)}) custom-call(s32[1]{0:T(128)} %bitcast.ex_ref, f32[16,128]{1,0:T(8,128)S(1)} %get-tuple-element.38.scale_ref, s32[256,128]{1,0:T(8,128)S(1)} %broadcast_in_dim.15.sampled_ref, bf16[2048,2048]{1,0:T(8,128)(2,1)S(1)} %copy-done), custom_call_target="tpu_custom_call" | custom-call | tf_op jit(solution)/shard_map/second_terms/pallas_call | solution.py:30
  42.9 3.4 %collective-permute-done.16.scale2_ref = f32[16,128]{1,0:T(8,128)S(1)} collective-permute-done((f32[16,128]{1,0:T(8,128)S(1)}, f32[16,128]{1,0:T(8,128)S(1)}, u32[]{:S(2)}, u32[]{:S(2)}) %collective-permute-start.16) | collective-permute-done | bytes 8224 | tf_op jit(solution)/shard_map/ppermute | solution.py:25
  46.4 2.9 %pair_terms.1 = (bf16[512,256]{1,0:T(8,128)(2,1)S(1)}, f32[256,256]{1,0:T(8,128)S(1)}, f32[128,256]{1,0:T(8,128)S(1)}, f32[128,256]{1,0:T(8,128)S(1)}) custom-call(s32[1]{0:T(128)} %bitcast.ex_ref, f32[16,128]{1,0:T(8,128)S(1)} %get-tuple-element.38.scale_ref, f32[16,128]{1,0:T(8,128)S(1)} %collective-permute-done.16.scale2_ref, ...), custom_call_target="tpu_custom_call" | custom-call | tf_op jit(solution)/shard_map/pair_terms/pallas_call | solution.py:30
  49.3 1.6 %collective-permute-start.17 = (bf16[512,256]{1,0:T(8,128)(2,1)S(1)}, bf16[512,256]{1,0:T(8,128)(2,1)S(1)}, u32[]{:S(2)}, u32[]{:S(2)}) collective-permute-start(bf16[512,256]{1,0:T(8,128)(2,1)S(1)} %get-tuple-element.40), channel_id=1, source_target_pairs={{0,8},{4,12},{8,0},{12,4},{16,24},{20,28},{24,16},{28,20},{1,9},{5... | collective-permute-start | bytes 786440 | tf_op jit(solution)/shard_map/ppermute | solution.py:25
  52.0 4.8 %third_terms.1 = (f32[128,1536]{1,0:T(8,128)S(1)}, bf16[128,1536]{1,0:T(8,128)(2,1)S(1)}, f32[128,1536]{1,0:T(8,128)S(1)}, bf16[128,1536]{1,0:T(8,128)(2,1)S(1)}, f32[128,1536]{1,0:T(8,128)S(1)}) custom-call(s32[1]{0:T(128)} %bitcast.ex_ref, f32[16,128]{1,0:T(8,128)S(1)} %get-tuple-element.38.scale_ref, s32[640,128]{1,0:T(8,128)S(1)} %broadcast_in_dim.16.sampled_ref, ...), custom_call_target="tpu_custom_call" | custom-call | tf_op jit(solution)/shard_map/third_terms/pallas_call | solution.py:30
  56.8 3.2 %collective-permute-done.17 = bf16[512,256]{1,0:T(8,128)(2,1)S(1)} collective-permute-done((bf16[512,256]{1,0:T(8,128)(2,1)S(1)}, bf16[512,256]{1,0:T(8,128)(2,1)S(1)}, u32[]{:S(2)}, u32[]{:S(2)}) %collective-permute-start.17) | collective-permute-done | bytes 262176 | tf_op jit(solution)/shard_map/ppermute | solution.py:25
  60.2 4.4 %collective-permute-done.8 = bf16[128,1536]{1,0:T(8,128)(2,1)S(1)} collective-permute-done((bf16[128,1536]{1,0:T(8,128)(2,1)S(1)}, bf16[128,1536]{1,0:T(8,128)(2,1)S(1)}, u32[]{:S(2)}, u32[]{:S(2)}) %collective-permute-start.8) | collective-permute-done | bytes 393248 | tf_op jit(solution)/shard_map/ppermute | solution.py:25
  66.7 1.9 %collective-permute-start.13 = (bf16[128,1536]{1,0:T(8,128)(2,1)S(1)}, bf16[128,1536]{1,0:T(8,128)(2,1)S(1)}, u32[]{:S(2)}, u32[]{:S(2)}) collective-permute-start(bf16[128,1536]{1,0:T(8,128)(2,1)S(1)} %get-tuple-element.37), channel_id=1, source_target_pairs={{0,4},{4,0},{8,12},{12,8},{16,20},{20,16},{24,28},{28,24},{1,5},{5... | collective-permute-start | bytes 1179656 | tf_op jit(solution)/shard_map/ppermute | solution.py:25
  68.5 2.5 %collective-permute-start.15 = (bf16[128,1536]{1,0:T(8,128)(2,1)S(1)}, bf16[128,1536]{1,0:T(8,128)(2,1)S(1)}, u32[]{:S(2)}, u32[]{:S(2)}) collective-permute-start(bf16[128,1536]{1,0:T(8,128)(2,1)S(1)} %convert_add_fusion.1), channel_id=1, source_target_pairs={{0,16},{4,20},{8,24},{12,28},{16,0},{20,4},{24,8},{28,12},{1,17},{... | collective-permute-start | bytes 1179656 | tf_op jit(solution)/shard_map/ppermute | solution.py:25
  71.1 2.0 %collective-permute-done.9 = f32[1024]{0:T(1024)S(1)} collective-permute-done((f32[1024]{0:T(1024)S(1)}, f32[1024]{0:T(1024)S(1)}, u32[]{:S(2)}, u32[]{:S(2)}) %collective-permute-start.9) | collective-permute-done | bytes 4128 | tf_op jit(solution)/shard_map/ppermute | solution.py:25
  73.5 3.2 %collective-permute-done.10 = f32[512]{0:T(512)S(1)} collective-permute-done((f32[512]{0:T(512)S(1)}, f32[512]{0:T(512)S(1)}, u32[]{:S(2)}, u32[]{:S(2)}) %collective-permute-start.10) | collective-permute-done | bytes 2080 | tf_op jit(solution)/shard_map/ppermute | solution.py:25
  77.1 5.5 %collective-permute-done.13 = bf16[128,1536]{1,0:T(8,128)(2,1)S(1)} collective-permute-done((bf16[128,1536]{1,0:T(8,128)(2,1)S(1)}, bf16[128,1536]{1,0:T(8,128)(2,1)S(1)}, u32[]{:S(2)}, u32[]{:S(2)}) %collective-permute-start.13) | collective-permute-done | bytes 393248 | tf_op jit(solution)/shard_map/ppermute | solution.py:25
  82.7 1.7 %collective-permute-start.14 = (bf16[128,1536]{1,0:T(8,128)(2,1)S(1)}, bf16[128,1536]{1,0:T(8,128)(2,1)S(1)}, u32[]{:S(2)}, u32[]{:S(2)}) collective-permute-start(bf16[128,1536]{1,0:T(8,128)(2,1)S(1)} %add_convert_fusion), channel_id=1, source_target_pairs={{0,8},{4,12},{8,0},{12,4},{16,24},{20,28},{24,16},{28,20},{1,9},{5... | collective-permute-start | bytes 1179656 | tf_op jit(solution)/shard_map/ppermute | solution.py:25
  85.1 7.7 %collective-permute-done.14 = bf16[128,1536]{1,0:T(8,128)(2,1)S(1)} collective-permute-done((bf16[128,1536]{1,0:T(8,128)(2,1)S(1)}, bf16[128,1536]{1,0:T(8,128)(2,1)S(1)}, u32[]{:S(2)}, u32[]{:S(2)}) %collective-permute-start.14) | collective-permute-done | bytes 393248 | tf_op jit(solution)/shard_map/ppermute | solution.py:25
  (76 shorter events, 15.9 us)
Async XLA Ops:
  0.6 26.3 %copy-start.1 = (f32[2048]{0:T(1024)S(1)}, f32[2048]{0:T(1024)}, u32[]{:S(2)}) copy-start(f32[2048]{0:T(1024)} %param.9) | copy-start | bytes 24580
  0.6 26.3 %copy-start.3 = (s32[2048]{0:T(1024)S(1)}, s32[2048]{0:T(1024)}, u32[]{:S(2)}) copy-start(s32[2048]{0:T(1024)} %param.8) | copy-start | bytes 24580
  0.7 26.3 %copy-start.2 = (s32[2048]{0:T(1024)S(1)}, s32[2048]{0:T(1024)}, u32[]{:S(2)}) copy-start(s32[2048]{0:T(1024)} %param.7) | copy-start | bytes 24580
  1.4 6.1 %collective-permute-start = (bf16[256]{0:T(256)(128)(2,1)S(1)}, bf16[256]{0:T(256)(128)(2,1)S(1)}, u32[]{:S(2)}, u32[]{:S(2)}) collective-permute-start(bf16[256]{0:T(256)(128)(2,1)S(1)} %convert_element_type.51), channel_id=1, source_target_pairs={{0,4},{4,0},{8,12},{12,8},{16,20},{20,16},{24,28},{28,24},{1,5},{5... | collective-permute-start | bytes 1544 | tf_op jit(solution)/shard_map/ppermute | solution.py:25
  8.1 3.6 %collective-permute-start.1 = (bf16[512]{0:T(512)(128)(2,1)S(1)}, bf16[512]{0:T(512)(128)(2,1)S(1)}, u32[]{:S(2)}, u32[]{:S(2)}) collective-permute-start(bf16[512]{0:T(512)(128)(2,1)S(1)} %pad_maximum_fusion.2), channel_id=1, source_target_pairs={{0,8},{4,12},{8,0},{12,4},{16,24},{20,28},{24,16},{28,20},{1,9},{5... | collective-permute-start | bytes 3080 | tf_op jit(solution)/shard_map/ppermute | solution.py:25
  11.8 4.5 %collective-permute-start.2 = (bf16[1024]{0:T(1024)(128)(2,1)S(1)}, bf16[1024]{0:T(1024)(128)(2,1)S(1)}, u32[]{:S(2)}, u32[]{:S(2)}) collective-permute-start(bf16[1024]{0:T(1024)(128)(2,1)S(1)} %pad_maximum_fusion.1), channel_id=1, source_target_pairs={{0,16},{4,20},{8,24},{12,28},{16,0},{20,4},{24,8},{28,12},{1,17},{... | collective-permute-start | bytes 6152 | tf_op jit(solution)/shard_map/ppermute | solution.py:25
  14.5 26.1 %collective-permute-start.5 = (bf16[2048,256]{1,0:T(8,128)(2,1)S(1)}, bf16[2048,256]{1,0:T(8,128)(2,1)S(1)}, u32[]{:S(2)}, u32[]{:S(2)}) collective-permute-start(bf16[2048,256]{1,0:T(8,128)(2,1)S(1)} %slice_select_fusion), channel_id=1, source_target_pairs={{0,4},{4,0},{8,12},{12,8},{16,20},{20,16},{24,28},{28,24},{1,5},{5... | collective-permute-start | bytes 3145736 | tf_op jit(solution)/shard_map/ppermute | solution.py:25
  16.4 3.4 %copy-start = (bf16[2048,2048]{1,0:T(8,128)(2,1)S(1)}, bf16[2048,2048]{1,0:T(8,128)(2,1)}, u32[]{:S(2)}) copy-start(bf16[2048,2048]{1,0:T(8,128)(2,1)} %pooled_ref.11) | copy-start | bytes 25165828
  22.0 1.2 %collective-permute-start.3 = (f32[16,128]{1,0:T(8,128)S(1)}, f32[16,128]{1,0:T(8,128)S(1)}, u32[]{:S(2)}, u32[]{:S(2)}) collective-permute-start(f32[16,128]{1,0:T(8,128)S(1)} %margins.1), channel_id=1, source_target_pairs={{0,1},{1,0},{2,3},{3,2},{4,5},{5,4},{6,7},{7,6},{8,9},{9,8},{10,11... | collective-permute-start | bytes 24584 | tf_op jit(solution)/shard_map/ppermute | solution.py:25
  23.2 3.7 %collective-permute-start.4 = (f32[16,128]{1,0:T(8,128)S(1)}, f32[16,128]{1,0:T(8,128)S(1)}, u32[]{:S(2)}, u32[]{:S(2)}) collective-permute-start(f32[16,128]{1,0:T(8,128)S(1)} %add.48.mine_ref), channel_id=1, source_target_pairs={{0,2},{1,3},{2,0},{3,1},{4,6},{5,7},{6,4},{7,5},{8,10},{9,11},{10,... | collective-permute-start | bytes 24584 | tf_op jit(solution)/shard_map/ppermute | solution.py:25
  29.0 22.0 %collective-permute-start.6 = (bf16[128,1536]{1,0:T(8,128)(2,1)S(1)}, bf16[128,1536]{1,0:T(8,128)(2,1)S(1)}, u32[]{:S(2)}, u32[]{:S(2)}) collective-permute-start(bf16[128,1536]{1,0:T(8,128)(2,1)S(1)} %get-tuple-element.29), channel_id=1, source_target_pairs={{0,4},{4,0},{8,12},{12,8},{16,20},{20,16},{24,28},{28,24},{1,5},{5... | collective-permute-start | bytes 1179656 | tf_op jit(solution)/shard_map/ppermute | solution.py:25
  29.4 16.8 %collective-permute-start.16 = (f32[16,128]{1,0:T(8,128)S(1)}, f32[16,128]{1,0:T(8,128)S(1)}, u32[]{:S(2)}, u32[]{:S(2)}) collective-permute-start(f32[16,128]{1,0:T(8,128)S(1)} %get-tuple-element.38.scale_ref), channel_id=1, source_target_pairs={{0,4},{4,0},{8,12},{12,8},{16,20},{20,16},{24,28},{28,24},{1,5},{5... | collective-permute-start | bytes 24584 | tf_op jit(solution)/shard_map/ppermute | solution.py:25
  49.3 10.7 %collective-permute-start.17 = (bf16[512,256]{1,0:T(8,128)(2,1)S(1)}, bf16[512,256]{1,0:T(8,128)(2,1)S(1)}, u32[]{:S(2)}, u32[]{:S(2)}) collective-permute-start(bf16[512,256]{1,0:T(8,128)(2,1)S(1)} %get-tuple-element.40), channel_id=1, source_target_pairs={{0,8},{4,12},{8,0},{12,4},{16,24},{20,28},{24,16},{28,20},{1,9},{5... | collective-permute-start | bytes 786440 | tf_op jit(solution)/shard_map/ppermute | solution.py:25
  51.1 13.6 %collective-permute-start.8 = (bf16[128,1536]{1,0:T(8,128)(2,1)S(1)}, bf16[128,1536]{1,0:T(8,128)(2,1)S(1)}, u32[]{:S(2)}, u32[]{:S(2)}) collective-permute-start(bf16[128,1536]{1,0:T(8,128)(2,1)S(1)} %convert_add_fusion.2), channel_id=1, source_target_pairs={{0,8},{4,12},{8,0},{12,4},{16,24},{20,28},{24,16},{28,20},{1,9},{5... | collective-permute-start | bytes 1179656 | tf_op jit(solution)/shard_map/ppermute | solution.py:25
  51.6 13.1 %collective-permute-start.7 = (bf16[128,1536]{1,0:T(8,128)(2,1)S(1)}, bf16[128,1536]{1,0:T(8,128)(2,1)S(1)}, u32[]{:S(2)}, u32[]{:S(2)}) collective-permute-start(bf16[128,1536]{1,0:T(8,128)(2,1)S(1)} %get-tuple-element.32), channel_id=1, source_target_pairs={{0,4},{4,0},{8,12},{12,8},{16,20},{20,16},{24,28},{28,24},{1,5},{5... | collective-permute-start | bytes 1179656 | tf_op jit(solution)/shard_map/ppermute | solution.py:25
  60.1 10.9 %collective-permute-start.18 = (bf16[256,256]{1,0:T(8,128)(2,1)S(1)}, bf16[256,256]{1,0:T(8,128)(2,1)S(1)}, u32[]{:S(2)}, u32[]{:S(2)}) collective-permute-start(bf16[256,256]{1,0:T(8,128)(2,1)S(1)} %fusion), channel_id=1, source_target_pairs={{0,16},{4,20},{8,24},{12,28},{16,0},{20,4},{24,8},{28,12},{1,17},{... | collective-permute-start | bytes 393224 | tf_op jit(solution)/shard_map/ppermute | solution.py:25
  66.0 7.0 %collective-permute-start.9 = (f32[1024]{0:T(1024)S(1)}, f32[1024]{0:T(1024)S(1)}, u32[]{:S(2)}, u32[]{:S(2)}) collective-permute-start(f32[1024]{0:T(1024)S(1)} %bitcast.51), channel_id=1, source_target_pairs={{0,16},{4,20},{8,24},{12,28},{16,0},{20,4},{24,8},{28,12},{1,17},{... | collective-permute-start | bytes 12296 | tf_op jit(solution)/shard_map/ppermute | solution.py:25
  66.5 18.6 %collective-permute-start.12 = (bf16[128,1536]{1,0:T(8,128)(2,1)S(1)}, bf16[128,1536]{1,0:T(8,128)(2,1)S(1)}, u32[]{:S(2)}, u32[]{:S(2)}) collective-permute-start(bf16[128,1536]{1,0:T(8,128)(2,1)S(1)} %get-tuple-element.35), channel_id=1, source_target_pairs={{0,4},{4,0},{8,12},{12,8},{16,20},{20,16},{24,28},{28,24},{1,5},{5... | collective-permute-start | bytes 1179656 | tf_op jit(solution)/shard_map/ppermute | solution.py:25
  66.7 15.9 %collective-permute-start.13 = (bf16[128,1536]{1,0:T(8,128)(2,1)S(1)}, bf16[128,1536]{1,0:T(8,128)(2,1)S(1)}, u32[]{:S(2)}, u32[]{:S(2)}) collective-permute-start(bf16[128,1536]{1,0:T(8,128)(2,1)S(1)} %get-tuple-element.37), channel_id=1, source_target_pairs={{0,4},{4,0},{8,12},{12,8},{16,20},{20,16},{24,28},{28,24},{1,5},{5... | collective-permute-start | bytes 1179656 | tf_op jit(solution)/shard_map/ppermute | solution.py:25
  68.5 16.5 %collective-permute-start.15 = (bf16[128,1536]{1,0:T(8,128)(2,1)S(1)}, bf16[128,1536]{1,0:T(8,128)(2,1)S(1)}, u32[]{:S(2)}, u32[]{:S(2)}) collective-permute-start(bf16[128,1536]{1,0:T(8,128)(2,1)S(1)} %convert_add_fusion.1), channel_id=1, source_target_pairs={{0,16},{4,20},{8,24},{12,28},{16,0},{20,4},{24,8},{28,12},{1,17},{... | collective-permute-start | bytes 1179656 | tf_op jit(solution)/shard_map/ppermute | solution.py:25
  73.0 3.6 %collective-permute-start.10 = (f32[512]{0:T(512)S(1)}, f32[512]{0:T(512)S(1)}, u32[]{:S(2)}, u32[]{:S(2)}) collective-permute-start(f32[512]{0:T(512)S(1)} %slice_select_fusion.1), channel_id=1, source_target_pairs={{0,8},{4,12},{8,0},{12,4},{16,24},{20,28},{24,16},{28,20},{1,9},{5... | collective-permute-start | bytes 6152 | tf_op jit(solution)/shard_map/ppermute | solution.py:25
  73.1 11.9 %collective-permute-start.19 = (bf16[128,256]{1,0:T(8,128)(2,1)S(1)}, bf16[128,256]{1,0:T(8,128)(2,1)S(1)}, u32[]{:S(2)}, u32[]{:S(2)}) collective-permute-start(bf16[128,256]{1,0:T(8,128)(2,1)S(1)} %fusion.1), channel_id=1, source_target_pairs={{0,4},{4,0},{8,12},{12,8},{16,20},{20,16},{24,28},{28,24},{1,5},{5... | collective-permute-start | bytes 196616 | tf_op jit(solution)/shard_map/ppermute | solution.py:25
  76.7 7.7 %collective-permute-start.11 = (f32[256]{0:T(256)S(1)}, f32[256]{0:T(256)S(1)}, u32[]{:S(2)}, u32[]{:S(2)}) collective-permute-start(f32[256]{0:T(256)S(1)} %broadcast_select_fusion.5), channel_id=1, source_target_pairs={{0,4},{4,0},{8,12},{12,8},{16,20},{20,16},{24,28},{28,24},{1,5},{5... | collective-permute-start | bytes 3080 | tf_op jit(solution)/shard_map/ppermute | solution.py:25
  82.7 10.1 %collective-permute-start.14 = (bf16[128,1536]{1,0:T(8,128)(2,1)S(1)}, bf16[128,1536]{1,0:T(8,128)(2,1)S(1)}, u32[]{:S(2)}, u32[]{:S(2)}) collective-permute-start(bf16[128,1536]{1,0:T(8,128)(2,1)S(1)} %add_convert_fusion), channel_id=1, source_target_pairs={{0,8},{4,12},{8,0},{12,4},{16,24},{20,28},{24,16},{28,20},{1,9},{5... | collective-permute-start | bytes 1179656 | tf_op jit(solution)/shard_map/ppermute | solution.py:25

commit v3 on v0

v3 whole, which is shorter than its diff:
```python
import functools
import math

import jax
import jax.numpy as jnp
from jax import lax
from jax.experimental import pallas as pl
from jax.experimental.pallas import tpu as pltpu
from jax.sharding import PartitionSpec as P

LANES = 128
PARAMS = pltpu.CompilerParams(vmem_limit_bytes=40 * 1024 * 1024)
NO_COST = pl.CostEstimate(flops=0, bytes_accessed=0, transcendentals=0)
ANY = pl.BlockSpec(memory_space=pl.ANY)
VMEM = pl.BlockSpec(memory_space=pltpu.VMEM)
SMEM = pl.BlockSpec(memory_space=pltpu.SMEM)


def tile_of(extent, most):
    size = most
    while extent % size:
        size //= 2
    return size


def swap_with(value, axis, distance):
    count = lax.axis_size(axis)
    return lax.ppermute(value, axis, [(i, i ^ distance) for i in range(count)])


def wide(value):
    return value.astype(jnp.float32)


def narrow(value):
    return value.astype(jnp.bfloat16)


def call(kernel, name, out_shape, scratch, *operands, scalars=(), whole=(), large=(), deps=()):
    large = [pltpu.with_memory_space_constraint(x, pltpu.VMEM) for x in large]
    used = len(scalars) + len(operands) + len(large) + len(whole)
    return pl.pallas_call(
        lambda *refs: kernel(*refs[:used], *refs[used + len(deps) :]),
        in_specs=[SMEM] * len(scalars) + [VMEM] * (len(operands) + len(large)) + [ANY] * (len(whole) + len(deps)),
        out_specs=[VMEM] * len(out_shape),
        out_shape=[jax.ShapeDtypeStruct(*entry) for entry in out_shape],
        scratch_shapes=scratch,
        compiler_params=PARAMS,
        cost_estimate=NO_COST,
        name=name,
    )(*scalars, *operands, *large, *whole, *deps)


def margins_kernel(pieces, ex_ref, dir_ref, pooled_ref, out_ref, ordered_ref):
    rows, cols = pooled_ref.shape
    tile, width = tile_of(rows, 512), cols // pieces
    lanes = dir_ref.shape[1]
    for at in range(dir_ref.shape[0]):
        piece = jnp.broadcast_to(dir_ref[at : at + 1, :], (8, lanes))
        r, part = divmod(at * lanes, width)
        place = pl.ds(pl.multiple_of((ex_ref[0] ^ r) * width + part, lanes), lanes) if pieces > 1 else slice(None)
        ordered_ref[:, place] = piece
    left = ordered_ref[...].astype(jnp.bfloat16)
    for at in range(0, rows, tile):
        row = lax.dot_general(
            left, pooled_ref[at : at + tile, :], (((1,), (1,)), ((), ())), preferred_element_type=jnp.float32
        )
        for part in range(0, tile, LANES):
            group = (at + part) // LANES
            out_ref[group : group + 1, :] = row[0:1, part : part + LANES]


def sampled_rows(sampled_ref, ex_index, blocks):
    columns = []
    for r in blocks:
        row = sampled_ref[pl.ds(ex_index ^ r, 1), :]
        columns.append(jnp.broadcast_to(row, (LANES, row.shape[1])).T)
    return columns[0] if len(columns) == 1 else jnp.concatenate(columns)


def fill_signs(signs_ref, sampled, ex_index):
    high_bits = signs_ref.shape[1].bit_length() - 1
    lane = lax.broadcasted_iota(jnp.int32, sampled.shape, 1)
    folded = (sampled & lane) ^ (lax.shift_right_logical(sampled, high_bits) & ex_index)
    for shift_by in (16, 8, 4, 2, 1):
        folded = folded ^ lax.shift_right_logical(folded, shift_by)
    tiles = [(1 - 2 * (folded & 1)).astype(jnp.float32)]
    for bit in range(LANES.bit_length() - 1, high_bits):
        flip = (1 - 2 * (lax.shift_right_logical(sampled, bit) & 1)).astype(jnp.float32)
        tiles = tiles + [tile * flip for tile in tiles]
    for at, tile in enumerate(tiles):
        signs_ref[:, at * LANES : (at + 1) * LANES] = tile.astype(jnp.bfloat16)


def fill_scale(scale_col_ref, scale):
    for at in range(scale.shape[0]):
        square = jnp.broadcast_to(scale[at : at + 1, :], (LANES, LANES))
        scale_col_ref[at * LANES : (at + 1) * LANES, :] = square.T


def weigh(pooled, scale_col):
    pieces = []
    for at in range(0, pooled.shape[1], LANES):
        part = pooled[:, at : at + LANES].astype(jnp.float32)
        pieces.append((part * scale_col).astype(jnp.bfloat16))
    return pieces[0] if len(pieces) == 1 else jnp.concatenate(pieces, axis=1)


def weights_kernel(mine_ref, theirs_ref, old_ref, labels_ref, bits_ref, margins_ref, scale_ref, residual_ref):
    margins = old_ref[...] + (mine_ref[...] + theirs_ref[...])
    up, down = jax.nn.sigmoid(margins), jax.nn.sigmoid(-margins)
    margins_ref[...] = margins
    scale_ref[...] = (2 * bits_ref[...] - 1).astype(jnp.float32) * jnp.sqrt(up * down)
    residual_ref[...] = up - labels_ref[...].astype(jnp.float32)


def terms_kernel(places, blocks, ex_ref, scale_ref, sampled_ref, pooled_ref, *rest):
    *outs, signs_ref, scale_col_ref = rest
    cols = pooled_ref.shape[1]
    tile = tile_of(cols, 256)
    fill_scale(scale_col_ref, scale_ref[...])
    fill_signs(signs_ref, sampled_rows(sampled_ref, ex_ref[0], blocks), ex_ref[0])
    for at in range(0, cols, tile):
        weighted = weigh(pooled_ref[:, at : at + tile], scale_col_ref[...])
        terms = jnp.dot(signs_ref[...], weighted, preferred_element_type=jnp.float32)
        for (row, col), out in zip(places, outs):
            if col <= at < col + out.shape[1]:
                out[:, at - col : at - col + tile] = terms[row : row + out.shape[0]].astype(out.dtype)


def terms_of(name, blocks, ex_scalar, scale, sampled, pooled, places, outs, deps=()):
    rows, block_rows = pooled.shape[0], sampled.shape[1]
    return call(
        functools.partial(terms_kernel, places, blocks),
        name,
        outs,
        [
            pltpu.VMEM((len(blocks) * block_rows, rows), jnp.bfloat16),
            pltpu.VMEM((rows, LANES), jnp.float32),
        ],
        scale,
        sampled,
        scalars=(ex_scalar,),
        large=(pooled,),
        deps=deps,
    )


def gradient_kernel(residual_ref, pooled_ref, out_ref):
    row = jnp.concatenate([residual_ref[at : at + 1, :] for at in range(residual_ref.shape[0])], axis=1)
    left = jnp.broadcast_to(row, (8, row.shape[1])).astype(jnp.bfloat16)
    tile = tile_of(pooled_ref.shape[1], 512)
    for at in range(0, pooled_ref.shape[1], tile):
        terms = jnp.dot(left, pooled_ref[:, at : at + tile], preferred_element_type=jnp.float32)
        out_ref[:, at : at + tile] = terms[0:1, :]


def finish_kernel(counts, scales, *refs):
    *ins, sketch_ref, gradient_ref = refs
    col = 0
    ins = list(ins)
    for count, offsets in counts:
        group, ins = ins[:count], ins[count:]
        width = group[0].shape[1]
        total = group[0][...]
        for ref, offset in zip(group[1:], offsets):
            total = total + wide(ref[:, offset : offset + width])
        sketch_ref[:, col : col + width] = total * scales[0]
        col += width
    gradient_ref[...] = (ins[-2][...] + ins[-1][...]) * scales[1]


def on_device(pooled, labels, sign_bits, margins_old, direction, sample_rows):
    rows, cols = pooled.shape
    ex_count, feat_count = lax.axis_size("ex"), lax.axis_size("feat")
    bits = ex_count.bit_length() - 1
    ex_index = lax.axis_index("ex").astype(jnp.int32)
    ex_scalar = ex_index.reshape(1)
    sketch_count = sample_rows.shape[0]
    block_rows = sketch_count // ex_count
    dense = (rows // LANES, LANES)
    sampled = sample_rows.reshape(ex_count, block_rows)
    pieces = ex_count if direction.shape[0] % LANES == 0 else 1
    step_dir = direction.reshape(-1, LANES) if pieces > 1 else direction
    for bit in range(bits):
        other = swap_with(step_dir, "ex", 1 << bit)
        if pieces > 1:
            step_dir = jnp.concatenate([step_dir, other])
        else:
            low = (ex_index >> bit) & 1 == 0
            step_dir = jnp.concatenate([jnp.where(low, step_dir, other), jnp.where(low, other, step_dir)])

    (terms,) = call(
        functools.partial(margins_kernel, pieces),
        "margins",
        [(dense, jnp.float32)],
        [pltpu.VMEM((8, cols), jnp.float32)],
        step_dir if pieces > 1 else step_dir.reshape(1, cols),
        scalars=(ex_scalar,),
        large=(pooled,),
    )
    mine, theirs = terms, jnp.zeros_like(terms)
    distance = 1
    while distance < feat_count:
        mine, theirs = terms, swap_with(terms, "feat", distance)
        terms = mine + theirs
        distance *= 2

    margins, scale, residual = call(
        weights_kernel,
        "weights",
        [(dense, jnp.float32)] * 3,
        [],
        mine,
        theirs,
        margins_old.reshape(dense),
        labels.reshape(dense),
        sign_bits.reshape(dense),
    )
    order = [[r for r in range(ex_count - 1, 0, -1) if r & ((2 << bit) - 1) == 1 << bit] for bit in range(bits)]
    first = order[0][:2]
    cut = cols // 2 // (2 * LANES) * (2 * LANES) or cols
    spans = [(0, cut), (cut, cols)] if cut < cols else [(0, cols)]
    made = terms_of(
        "first_terms",
        first,
        ex_scalar,
        scale,
        sampled,
        pooled,
        [(0, begin) for begin, _ in spans],
        [((len(first) * block_rows, end - begin), jnp.bfloat16) for begin, end in spans],
    )
    last = made
    arrived_first = [swap_with(x, "ex", 1) for x in made]

    (part,) = call(
        gradient_kernel,
        "gradient",
        [((1, cols), jnp.float32)],
        [],
        residual,
        large=(pooled,),
        deps=last[:1],
    )
    last = [part]
    part = part.reshape(-1)

    own, arrivals = {}, {r: [] for r in range(ex_count)}

    def more(blocks, name, deps):
        cuts = [(k, r, span) for k, r in enumerate(blocks) for span in (spans if r in parted else [(0, cols)])]
        made = terms_of(
            name,
            blocks,
            ex_scalar,
            scale,
            sampled,
            pooled,
            [(k * block_rows, begin) for k, _, (begin, _) in cuts],
            [((block_rows, end - begin), jnp.bfloat16 if r & 1 else jnp.float32) for _, r, (begin, end) in cuts],
            deps,
        )
        for (_, r, (begin, _)), value in zip(cuts, made):
            own.setdefault(r, {})[begin] = value

    second = [r ^ 1 for r in first]
    parted = second + [0]
    more(second + order[0][2:3], "second_terms", last)

    for k, r in enumerate(first):
        for (begin, _), value in zip(spans, arrived_first):
            arrivals[r ^ 1].append((value[k * block_rows : (k + 1) * block_rows], begin))

    def exchange(r, spans):
        bit = (r & -r).bit_length() - 1
        for begin, end in spans:
            total = own[r][begin] if begin in own[r] and own[r][begin].shape[1] == end - begin else own[r][0][:, begin:end]
            for value, offset in arrivals[r]:
                if offset <= begin < offset + value.shape[1]:
                    total = total + wide(value[:, begin - offset : end - offset])
            last = swap_with(narrow(total), "ex", 1 << bit)
            arrivals[r ^ (1 << bit)].append((last, begin))
        return last

    left = [r for r in range(ex_count - 1, -1, -1) if r not in own and r not in first]
    began = second[: bits - 1] if len(spans) > 1 else []
    for at, r in enumerate(began):
        last = exchange(r, spans[:1])
        now, left = (left, []) if at == len(began) - 1 else (left[:-1], left[-1:])
        if now:
            more(now, f"terms_{at}", [last])
    if left:
        more(left, "last_terms", ())
    for r in order[0]:
        if r not in first:
            exchange(r, [(0, cols)])
    for bit in range(1, bits):
        for r in order[bit]:
            if r in began:
                exchange(r, spans[1:])
            else:
                exchange(r, spans if any(x.shape[1] < cols for x, _ in arrivals[r]) else [(0, cols)])

    for bit in reversed(range(bits)):
        low = (ex_index >> bit) & 1 == 0
        lower, upper = jnp.split(part, 2)
        arrived = swap_with(jnp.where(low, upper, lower), "ex", 1 << bit)
        kept = jnp.where(low, lower, upper)
        part = kept + arrived
    ends, counts = [], []
    for begin, end in spans:
        group, offsets = [own[0][begin]], []
        for value, offset in arrivals[0]:
            if offset <= begin < offset + value.shape[1]:
                group.append(value)
                offsets.append(begin - offset)
        ends += group
        counts.append((len(group), offsets))
    sketch, gradient = call(
        functools.partial(
            finish_kernel, counts, (1 / math.sqrt(sketch_count), 1 / math.sqrt(rows * ex_count))
        ),
        "finish",
        [((block_rows, cols), jnp.float32), ((1, kept.shape[0]), jnp.float32)],
        [],
        *ends,
        kept.reshape(1, -1),
        arrived.reshape(1, -1),
    )
    return margins.reshape(rows), gradient.reshape(-1), sketch


def solution(mesh):
    return jax.shard_map(
        on_device,
        mesh=mesh,
        in_specs=(P("ex", "feat"), P("ex"), P("ex"), P("ex"), P(("feat", "ex")), P()),
        out_specs=(P("ex"), P(("feat", "ex")), P("ex", "feat")),
        check_vma=False,
    )
```

time: 216 us -> 86.3 us (0.40)
  waiting for transfers between devices: 121 us -> 25.5 us
  blocking collectives: 46.7 us -> 0 us
  starting transfers between devices: 0.04 us -> 29.6 us
  matrix products: 28.6 us -> 0 us
  Pallas kernels: 0 us -> 16.9 us
  between operations: 14.8 us -> 0.83 us
  local copies, waits for them, and re-layouts: 1.28 us -> 10.2 us
    reduce_scatter x1 -> x0, waiting for transfers between devices: 121 us -> none  [on_device(): lax.psum_scatter(jnp.dot(signs_table, weighted, preferred_element_type=jn...]
    ppermute x0 -> x17, starting transfers between devices: none -> 29.6 us  [swap_with(): return lax.ppermute(value, axis, [(i, i ^ distance) for i in range(count)])]
    dot_general x3 -> x0, matrix products: 28.6 us -> none  [the longest x1 17.9 us: on_device(): jnp.dot(signs_table, weighted, preferred_element_type=jnp.float32)]
    ppermute x0 -> x17, waiting for transfers between devices: none -> 25.5 us  [swap_with(): return lax.ppermute(value, axis, [(i, i ^ distance) for i in range(count)])]
    all_gather x1 -> x0, blocking collectives: 22.2 us -> none  [on_device(): lax.all_gather(direction.astype(jnp.bfloat16), 'ex', axis=0, tiled=True)]
    unnamed x1 -> x0, blocking collectives: 18.7 us -> none
    pallas_call x0 -> x8, Pallas kernels: none -> 16.9 us  [call(): pl.pallas_call(lambda *refs: kernel(*refs[:used], *refs[used + len(deps):...]
    unnamed x14 -> x16, local copies, waits for them, and re-layouts: 1.27 us -> 10.2 us
  transfers between devices with their start and end apart: 1 -> 17, of which waited for: 1 -> 8; matrix products, arithmetic and copies ran while one was open for 3% -> 1% of each run, Pallas kernels for 0% -> 12%
where the time goes in v3:
time: 86.3 us; the launch traced here: 85.6 us
  starting transfers between devices  29.6 us (34%)
  waiting for transfers between devices  25.5 us (30%)
  Pallas kernels  16.9 us (20%)
  local copies, waits for them, and re-layouts  10.2 us (12%)
  other arithmetic  2.58 us (3%)
    ppermute x17, starting transfers between devices, swap_with(): return lax.ppermute(value, axis, [(i, i ^ distance) for i in range(count)])  29.6 us
    ppermute x17, waiting for transfers between devices, swap_with(): return lax.ppermute(value, axis, [(i, i ^ distance) for i in range(count)])  25.5 us
    pallas_call x8, Pallas kernels, call(): pl.pallas_call(lambda *refs: kernel(*refs[:used], *refs[used + len(deps):...  16.9 us
    unnamed x16, local copies, waits for them, and re-layouts  10.2 us
    concatenate x3, other arithmetic, on_device(): step_dir = jnp.concatenate([step_dir, other])  2.06 us
  transfers between devices with their start and end apart: 17, of which 8 were waited for; matrix products, arithmetic and copies ran while one was open for 1% of the time, Pallas kernels for 12%

profile of v3, /device:TPU:0, one launch (start us, length us, event | category | flops | bytes accessed | tf_op | source)
XLA Modules:
  0.0 85.6 jit_solution(8059013079142898389)
XLA Ops:
  0.7 3.0 %collective-permute-start = (f32[2,128]{1,0:T(2,128)}, f32[2,128]{1,0:T(2,128)S(1)}, u32[]{:S(2)}, u32[]{:S(2)}) collective-permute-start(f32[2,128]{1,0:T(2,128)} %bitcast.22), channel_id=1, source_target_pairs={{0,4},{4,0},{8,12},{12,8},{16,20},{20,16},{24,28},{28,24},{1,5},{5... | collective-permute-start | bytes 3080 | tf_op jit(solution)/shard_map/ppermute | solution.py:28
  3.7 1.8 %collective-permute-done = f32[2,128]{1,0:T(2,128)S(1)} collective-permute-done((f32[2,128]{1,0:T(2,128)}, f32[2,128]{1,0:T(2,128)S(1)}, u32[]{:S(2)}, u32[]{:S(2)}) %collective-permute-start) | collective-permute-done | bytes 1056 | tf_op jit(solution)/shard_map/ppermute | solution.py:28
  6.1 2.1 %collective-permute-start.1 = (f32[4,128]{1,0:T(4,128)S(1)}, f32[4,128]{1,0:T(4,128)S(1)}, u32[]{:S(2)}, u32[]{:S(2)}) collective-permute-start(f32[4,128]{1,0:T(4,128)S(1)} %pad_maximum_fusion.2), channel_id=1, source_target_pairs={{0,8},{4,12},{8,0},{12,4},{16,24},{20,28},{24,16},{28,20},{1,9},{5... | collective-permute-start | bytes 6152 | tf_op jit(solution)/shard_map/ppermute | solution.py:28
  10.5 3.0 %collective-permute-start.2 = (f32[8,128]{1,0:T(8,128)S(1)}, f32[8,128]{1,0:T(8,128)S(1)}, u32[]{:S(2)}, u32[]{:S(2)}) collective-permute-start(f32[8,128]{1,0:T(8,128)S(1)} %pad_maximum_fusion.1), channel_id=1, source_target_pairs={{0,16},{4,20},{8,24},{12,28},{16,0},{20,4},{24,8},{28,12},{1,17},{... | collective-permute-start | bytes 12296 | tf_op jit(solution)/shard_map/ppermute | solution.py:28
  13.5 1.6 %collective-permute-done.2 = f32[8,128]{1,0:T(8,128)S(1)} collective-permute-done((f32[8,128]{1,0:T(8,128)S(1)}, f32[8,128]{1,0:T(8,128)S(1)}, u32[]{:S(2)}, u32[]{:S(2)}) %collective-permute-start.2) | collective-permute-done | bytes 4128 | tf_op jit(solution)/shard_map/ppermute | solution.py:28
  15.8 3.4 %copy-done = bf16[2048,2048]{1,0:T(8,128)(2,1)S(1)} copy-done((bf16[2048,2048]{1,0:T(8,128)(2,1)S(1)}, bf16[2048,2048]{1,0:T(8,128)(2,1)}, u32[]{:S(2)}) %copy-start) | copy-done | bytes 8388632
  19.2 2.3 %margins.1 = f32[16,128]{1,0:T(8,128)S(1)} custom-call(s32[1]{0:T(128)} %bitcast.refs_0_, f32[16,128]{1,0:T(8,128)S(1)} %pad_maximum_fusion.refs_1_, bf16[2048,2048]{1,0:T(8,128)(2,1)S(1)} %copy-done), custom_call_target="tpu_custom_call" | custom-call | tf_op jit(solution)/shard_map/margins/pallas_call | solution.py:42
  22.6 1.9 %collective-permute-start.4 = (f32[16,128]{1,0:T(8,128)S(1)}, f32[16,128]{1,0:T(8,128)S(1)}, u32[]{:S(2)}, u32[]{:S(2)}) collective-permute-start(f32[16,128]{1,0:T(8,128)S(1)} %add.30.refs_0_), channel_id=1, source_target_pairs={{0,2},{1,3},{2,0},{3,1},{4,6},{5,7},{6,4},{7,5},{8,10},{9,11},{10,... | collective-permute-start | bytes 24584 | tf_op jit(solution)/shard_map/ppermute | solution.py:28
  24.5 1.8 %collective-permute-done.4.refs_1_ = f32[16,128]{1,0:T(8,128)S(1)} collective-permute-done((f32[16,128]{1,0:T(8,128)S(1)}, f32[16,128]{1,0:T(8,128)S(1)}, u32[]{:S(2)}, u32[]{:S(2)}) %collective-permute-start.4) | collective-permute-done | bytes 8224 | tf_op jit(solution)/shard_map/ppermute | solution.py:28
  26.9 2.7 %first_terms.1 = (bf16[256,1024]{1,0:T(8,128)(2,1)S(1)}, bf16[256,1024]{1,0:T(8,128)(2,1)S(1)}) custom-call(s32[1]{0:T(128)} %bitcast.refs_0_, f32[16,128]{1,0:T(8,128)S(1)} %get-tuple-element.20.refs_1_, s32[8,128]{1,0:T(8,128)S(1)} %bitcast.12, bf16[2048,2048]{1,0:T(8,128)(2,1)S(1)} %copy-done.1), custom_call_target="tpu_custom_call" | custom-call | tf_op jit(solution)/shard_map/first_terms/pallas_call | solution.py:42
  29.6 1.9 %collective-permute-start.11 = (bf16[256,1024]{1,0:T(8,128)(2,1)S(1)}, bf16[256,1024]{1,0:T(8,128)(2,1)S(1)}, u32[]{:S(2)}, u32[]{:S(2)}) collective-permute-start(bf16[256,1024]{1,0:T(8,128)(2,1)S(1)} %get-tuple-element.31), channel_id=1, source_target_pairs={{0,4},{4,0},{8,12},{12,8},{16,20},{20,16},{24,28},{28,24},{1,5},{5... | collective-permute-start | bytes 1572872 | tf_op jit(solution)/shard_map/ppermute | solution.py:28
  31.7 3.4 %copy-done.2 = bf16[2048,2048]{1,0:T(8,128)(2,1)S(1)} copy-done((bf16[2048,2048]{1,0:T(8,128)(2,1)S(1)}, bf16[2048,2048]{1,0:T(8,128)(2,1)}, u32[]{:S(2)}) %copy-start.2) | copy-done | bytes 8388632
  36.3 3.0 %collective-permute-start.14 = (f32[1024]{0:T(1024)S(1)}, f32[1024]{0:T(1024)S(1)}, u32[]{:S(2)}, u32[]{:S(2)}) collective-permute-start(f32[1024]{0:T(1024)S(1)} %bitcast.26), channel_id=1, source_target_pairs={{0,16},{4,20},{8,24},{12,28},{16,0},{20,4},{24,8},{28,12},{1,17},{... | collective-permute-start | bytes 12296 | tf_op jit(solution)/shard_map/ppermute | solution.py:28
  39.3 3.4 %copy-done.3 = bf16[2048,2048]{1,0:T(8,128)(2,1)S(1)} copy-done((bf16[2048,2048]{1,0:T(8,128)(2,1)S(1)}, bf16[2048,2048]{1,0:T(8,128)(2,1)}, u32[]{:S(2)}) %copy-start.3) | copy-done | bytes 8388632
  42.7 4.1 %second_terms.1 = (f32[128,1024]{1,0:T(8,128)S(1)}, f32[128,1024]{1,0:T(8,128)S(1)}, f32[128,1024]{1,0:T(8,128)S(1)}, f32[128,1024]{1,0:T(8,128)S(1)}, bf16[128,2048]{1,0:T(8,128)(2,1)S(1)}) custom-call(s32[1]{0:T(128)} %bitcast.refs_0_, f32[16,128]{1,0:T(8,128)S(1)} %get-tuple-element.20.refs_1_, s32[8,128]{1,0:T(8,128)S(1)} %bitcast.13, ...), custom_call_target="tpu_custom_call" | custom-call | tf_op jit(solution)/shard_map/second_terms/pallas_call | solution.py:42
  48.4 1.6 %collective-permute-start.12 = (bf16[128,1024]{1,0:T(8,128)(2,1)S(1)}, bf16[128,1024]{1,0:T(8,128)(2,1)S(1)}, u32[]{:S(2)}, u32[]{:S(2)}) collective-permute-start(bf16[128,1024]{1,0:T(8,128)(2,1)S(1)} %add_convert_fusion.2), channel_id=1, source_target_pairs={{0,8},{4,12},{8,0},{12,4},{16,24},{20,28},{24,16},{28,20},{1,9},{5... | collective-permute-start | bytes 786440 | tf_op jit(solution)/shard_map/ppermute | solution.py:28
  50.1 5.7 %collective-permute-done.5 = bf16[256,1024]{1,0:T(8,128)(2,1)S(1)} collective-permute-done((bf16[256,1024]{1,0:T(8,128)(2,1)S(1)}, bf16[256,1024]{1,0:T(8,128)(2,1)S(1)}, u32[]{:S(2)}, u32[]{:S(2)}) %collective-permute-start.5) | collective-permute-done | bytes 524320 | tf_op jit(solution)/shard_map/ppermute | solution.py:28
  55.9 2.0 %collective-permute-start.6 = (bf16[128,1024]{1,0:T(8,128)(2,1)S(1)}, bf16[128,1024]{1,0:T(8,128)(2,1)S(1)}, u32[]{:S(2)}, u32[]{:S(2)}) collective-permute-start(bf16[128,1024]{1,0:T(8,128)(2,1)S(1)} %add_convert_fusion.4), channel_id=1, source_target_pairs={{0,8},{4,12},{8,0},{12,4},{16,24},{20,28},{24,16},{28,20},{1,9},{5... | collective-permute-start | bytes 786440 | tf_op jit(solution)/shard_map/ppermute | solution.py:28
  58.1 3.0 %collective-permute-start.13 = (bf16[128,1024]{1,0:T(8,128)(2,1)S(1)}, bf16[128,1024]{1,0:T(8,128)(2,1)S(1)}, u32[]{:S(2)}, u32[]{:S(2)}) collective-permute-start(bf16[128,1024]{1,0:T(8,128)(2,1)S(1)} %add_convert_fusion.1), channel_id=1, source_target_pairs={{0,16},{4,20},{8,24},{12,28},{16,0},{20,4},{24,8},{28,12},{1,17},{... | collective-permute-start | bytes 786440 | tf_op jit(solution)/shard_map/ppermute | solution.py:28
  61.1 4.7 %collective-permute-done.6.refs_4_ = bf16[128,1024]{1,0:T(8,128)(2,1)S(1)} collective-permute-done((bf16[128,1024]{1,0:T(8,128)(2,1)S(1)}, bf16[128,1024]{1,0:T(8,128)(2,1)S(1)}, u32[]{:S(2)}, u32[]{:S(2)}) %collective-permute-start.6) | collective-permute-done | bytes 262176 | tf_op jit(solution)/shard_map/ppermute | solution.py:28
  65.8 2.9 %terms_0.1 = (f32[128,2048]{1,0:T(8,128)S(1)}, bf16[128,2048]{1,0:T(8,128)(2,1)S(1)}) custom-call(s32[1]{0:T(128)} %bitcast.refs_0_, f32[16,128]{1,0:T(8,128)S(1)} %get-tuple-element.20.refs_1_, s32[8,128]{1,0:T(8,128)S(1)} %bitcast.14, bf16[2048,2048]{1,0:T(8,128)(2,1)S(1)} %copy-done.3, bf16[128,1024]{1,0:T(8,128)(2,1)S(1)} %collective-permute-done.6.refs_4_), custom_call_target="tpu_custom_call" | custom-call | tf_op jit(solution)/shard_map/terms_0/pallas_call | solution.py:42
  70.8 3.8 %collective-permute-start.7 = (bf16[128,1024]{1,0:T(8,128)(2,1)S(1)}, bf16[128,1024]{1,0:T(8,128)(2,1)S(1)}, u32[]{:S(2)}, u32[]{:S(2)}) collective-permute-start(bf16[128,1024]{1,0:T(8,128)(2,1)S(1)} %add_convert_fusion.3), channel_id=1, source_target_pairs={{0,16},{4,20},{8,24},{12,28},{16,0},{20,4},{24,8},{28,12},{1,17},{... | collective-permute-start | bytes 786440 | tf_op jit(solution)/shard_map/ppermute | solution.py:28
  75.2 7.2 %collective-permute-done.7.refs_4_.refs_1_ = bf16[128,1024]{1,0:T(8,128)(2,1)S(1)} collective-permute-done((bf16[128,1024]{1,0:T(8,128)(2,1)S(1)}, bf16[128,1024]{1,0:T(8,128)(2,1)S(1)}, u32[]{:S(2)}, u32[]{:S(2)}) %collective-permute-start.7) | collective-permute-done | bytes 262176 | tf_op jit(solution)/shard_map/ppermute | solution.py:28
  82.4 1.9 %terms_1.1 = (f32[128,1024]{1,0:T(8,128)S(1)}, f32[128,1024]{1,0:T(8,128)S(1)}) custom-call(s32[1]{0:T(128)} %bitcast.refs_0_, f32[16,128]{1,0:T(8,128)S(1)} %get-tuple-element.20.refs_1_, s32[8,128]{1,0:T(8,128)S(1)} %bitcast.15, bf16[2048,2048]{1,0:T(8,128)(2,1)S(1)} %copy-done.3, bf16[128,1024]{1,0:T(8,128)(2,1)S(1)} %collective-permute-done.7.refs_4_.refs_1_), custom_call_target="tpu_custom_call" | custom-call | tf_op jit(solution)/shard_map/terms_1/pallas_call | solution.py:42
  (48 shorter events, 12.7 us)
Async XLA Ops:
  0.6 25.6 %copy-start.5 = (f32[2048]{0:T(1024)S(1)}, f32[2048]{0:T(1024)}, u32[]{:S(2)}) copy-start(f32[2048]{0:T(1024)} %param.9) | copy-start | bytes 24580
  0.6 25.6 %copy-start.7 = (s32[2048]{0:T(1024)S(1)}, s32[2048]{0:T(1024)}, u32[]{:S(2)}) copy-start(s32[2048]{0:T(1024)} %param.8) | copy-start | bytes 24580
  0.7 25.6 %copy-start.6 = (s32[2048]{0:T(1024)S(1)}, s32[2048]{0:T(1024)}, u32[]{:S(2)}) copy-start(s32[2048]{0:T(1024)} %param.7) | copy-start | bytes 24580
  0.7 26.2 %copy-start.4 = (s32[1024]{0:T(1024)S(1)}, s32[1024]{0:T(1024)}, u32[]{:S(2)}) copy-start(s32[1024]{0:T(1024)} %param.11) | copy-start | bytes 12292
  0.7 4.8 %collective-permute-start = (f32[2,128]{1,0:T(2,128)}, f32[2,128]{1,0:T(2,128)S(1)}, u32[]{:S(2)}, u32[]{:S(2)}) collective-permute-start(f32[2,128]{1,0:T(2,128)} %bitcast.22), channel_id=1, source_target_pairs={{0,4},{4,0},{8,12},{12,8},{16,20},{20,16},{24,28},{28,24},{1,5},{5... | collective-permute-start | bytes 3080 | tf_op jit(solution)/shard_map/ppermute | solution.py:28
  6.1 3.7 %collective-permute-start.1 = (f32[4,128]{1,0:T(4,128)S(1)}, f32[4,128]{1,0:T(4,128)S(1)}, u32[]{:S(2)}, u32[]{:S(2)}) collective-permute-start(f32[4,128]{1,0:T(4,128)S(1)} %pad_maximum_fusion.2), channel_id=1, source_target_pairs={{0,8},{4,12},{8,0},{12,4},{16,24},{20,28},{24,16},{28,20},{1,9},{5... | collective-permute-start | bytes 6152 | tf_op jit(solution)/shard_map/ppermute | solution.py:28
  10.5 4.6 %collective-permute-start.2 = (f32[8,128]{1,0:T(8,128)S(1)}, f32[8,128]{1,0:T(8,128)S(1)}, u32[]{:S(2)}, u32[]{:S(2)}) collective-permute-start(f32[8,128]{1,0:T(8,128)S(1)} %pad_maximum_fusion.1), channel_id=1, source_target_pairs={{0,16},{4,20},{8,24},{12,28},{16,0},{20,4},{24,8},{28,12},{1,17},{... | collective-permute-start | bytes 12296 | tf_op jit(solution)/shard_map/ppermute | solution.py:28
  15.8 3.4 %copy-start = (bf16[2048,2048]{1,0:T(8,128)(2,1)S(1)}, bf16[2048,2048]{1,0:T(8,128)(2,1)}, u32[]{:S(2)}) copy-start(bf16[2048,2048]{1,0:T(8,128)(2,1)} %refs_3_.7) | copy-start | bytes 25165828
  19.2 7.7 %copy-start.1 = (bf16[2048,2048]{1,0:T(8,128)(2,1)S(1)}, bf16[2048,2048]{1,0:T(8,128)(2,1)}, u32[]{:S(2)}) copy-start(bf16[2048,2048]{1,0:T(8,128)(2,1)} %refs_3_.7) | copy-start | bytes 25165828
  21.4 1.2 %collective-permute-start.3 = (f32[16,128]{1,0:T(8,128)S(1)}, f32[16,128]{1,0:T(8,128)S(1)}, u32[]{:S(2)}, u32[]{:S(2)}) collective-permute-start(f32[16,128]{1,0:T(8,128)S(1)} %margins.1), channel_id=1, source_target_pairs={{0,1},{1,0},{2,3},{3,2},{4,5},{5,4},{6,7},{7,6},{8,9},{9,8},{10,11... | collective-permute-start | bytes 24584 | tf_op jit(solution)/shard_map/ppermute | solution.py:28
  22.6 3.7 %collective-permute-start.4 = (f32[16,128]{1,0:T(8,128)S(1)}, f32[16,128]{1,0:T(8,128)S(1)}, u32[]{:S(2)}, u32[]{:S(2)}) collective-permute-start(f32[16,128]{1,0:T(8,128)S(1)} %add.30.refs_0_), channel_id=1, source_target_pairs={{0,2},{1,3},{2,0},{3,1},{4,6},{5,7},{6,4},{7,5},{8,10},{9,11},{10,... | collective-permute-start | bytes 24584 | tf_op jit(solution)/shard_map/ppermute | solution.py:28
  29.6 18.7 %collective-permute-start.11 = (bf16[256,1024]{1,0:T(8,128)(2,1)S(1)}, bf16[256,1024]{1,0:T(8,128)(2,1)S(1)}, u32[]{:S(2)}, u32[]{:S(2)}) collective-permute-start(bf16[256,1024]{1,0:T(8,128)(2,1)S(1)} %get-tuple-element.31), channel_id=1, source_target_pairs={{0,4},{4,0},{8,12},{12,8},{16,20},{20,16},{24,28},{28,24},{1,5},{5... | collective-permute-start | bytes 1572872 | tf_op jit(solution)/shard_map/ppermute | solution.py:28
  31.5 24.3 %collective-permute-start.5 = (bf16[256,1024]{1,0:T(8,128)(2,1)S(1)}, bf16[256,1024]{1,0:T(8,128)(2,1)S(1)}, u32[]{:S(2)}, u32[]{:S(2)}) collective-permute-start(bf16[256,1024]{1,0:T(8,128)(2,1)S(1)} %get-tuple-element.22.refs_2_), channel_id=1, source_target_pairs={{0,4},{4,0},{8,12},{12,8},{16,20},{20,16},{24,28},{28,24},{1,5},{5... | collective-permute-start | bytes 1572872 | tf_op jit(solution)/shard_map/ppermute | solution.py:28
  31.7 3.4 %copy-start.2 = (bf16[2048,2048]{1,0:T(8,128)(2,1)S(1)}, bf16[2048,2048]{1,0:T(8,128)(2,1)}, u32[]{:S(2)}) copy-start(bf16[2048,2048]{1,0:T(8,128)(2,1)} %refs_3_.7) | copy-start | bytes 25165828
  36.3 12.0 %collective-permute-start.14 = (f32[1024]{0:T(1024)S(1)}, f32[1024]{0:T(1024)S(1)}, u32[]{:S(2)}, u32[]{:S(2)}) collective-permute-start(f32[1024]{0:T(1024)S(1)} %bitcast.26), channel_id=1, source_target_pairs={{0,16},{4,20},{8,24},{12,28},{16,0},{20,4},{24,8},{28,12},{1,17},{... | collective-permute-start | bytes 12296 | tf_op jit(solution)/shard_map/ppermute | solution.py:28
  46.8 21.9 %collective-permute-start.9 = (bf16[128,2048]{1,0:T(8,128)(2,1)S(1)}, bf16[128,2048]{1,0:T(8,128)(2,1)S(1)}, u32[]{:S(2)}, u32[]{:S(2)}) collective-permute-start(bf16[128,2048]{1,0:T(8,128)(2,1)S(1)} %get-tuple-element.28), channel_id=1, source_target_pairs={{0,4},{4,0},{8,12},{12,8},{16,20},{20,16},{24,28},{28,24},{1,5},{5... | collective-permute-start | bytes 1572872 | tf_op jit(solution)/shard_map/ppermute | solution.py:28
  48.4 9.5 %collective-permute-start.12 = (bf16[128,1024]{1,0:T(8,128)(2,1)S(1)}, bf16[128,1024]{1,0:T(8,128)(2,1)S(1)}, u32[]{:S(2)}, u32[]{:S(2)}) collective-permute-start(bf16[128,1024]{1,0:T(8,128)(2,1)S(1)} %add_convert_fusion.2), channel_id=1, source_target_pairs={{0,8},{4,12},{8,0},{12,4},{16,24},{20,28},{24,16},{28,20},{1,9},{5... | collective-permute-start | bytes 786440 | tf_op jit(solution)/shard_map/ppermute | solution.py:28
  55.9 9.9 %collective-permute-start.6 = (bf16[128,1024]{1,0:T(8,128)(2,1)S(1)}, bf16[128,1024]{1,0:T(8,128)(2,1)S(1)}, u32[]{:S(2)}, u32[]{:S(2)}) collective-permute-start(bf16[128,1024]{1,0:T(8,128)(2,1)S(1)} %add_convert_fusion.4), channel_id=1, source_target_pairs={{0,8},{4,12},{8,0},{12,4},{16,24},{20,28},{24,16},{28,20},{1,9},{5... | collective-permute-start | bytes 786440 | tf_op jit(solution)/shard_map/ppermute | solution.py:28
  57.9 16.7 %collective-permute-start.15 = (f32[512]{0:T(512)S(1)}, f32[512]{0:T(512)S(1)}, u32[]{:S(2)}, u32[]{:S(2)}) collective-permute-start(f32[512]{0:T(512)S(1)} %slice_select_fusion), channel_id=1, source_target_pairs={{0,8},{4,12},{8,0},{12,4},{16,24},{20,28},{24,16},{28,20},{1,9},{5... | collective-permute-start | bytes 6152 | tf_op jit(solution)/shard_map/ppermute | solution.py:28
  58.1 26.3 %collective-permute-start.13 = (bf16[128,1024]{1,0:T(8,128)(2,1)S(1)}, bf16[128,1024]{1,0:T(8,128)(2,1)S(1)}, u32[]{:S(2)}, u32[]{:S(2)}) collective-permute-start(bf16[128,1024]{1,0:T(8,128)(2,1)S(1)} %add_convert_fusion.1), channel_id=1, source_target_pairs={{0,16},{4,20},{8,24},{12,28},{16,0},{20,4},{24,8},{28,12},{1,17},{... | collective-permute-start | bytes 786440 | tf_op jit(solution)/shard_map/ppermute | solution.py:28
  68.8 15.5 %collective-permute-start.10 = (bf16[128,2048]{1,0:T(8,128)(2,1)S(1)}, bf16[128,2048]{1,0:T(8,128)(2,1)S(1)}, u32[]{:S(2)}, u32[]{:S(2)}) collective-permute-start(bf16[128,2048]{1,0:T(8,128)(2,1)S(1)} %add_convert_fusion), channel_id=1, source_target_pairs={{0,8},{4,12},{8,0},{12,4},{16,24},{20,28},{24,16},{28,20},{1,9},{5... | collective-permute-start | bytes 1572872 | tf_op jit(solution)/shard_map/ppermute | solution.py:28
  69.1 15.3 %collective-permute-start.8 = (bf16[128,2048]{1,0:T(8,128)(2,1)S(1)}, bf16[128,2048]{1,0:T(8,128)(2,1)S(1)}, u32[]{:S(2)}, u32[]{:S(2)}) collective-permute-start(bf16[128,2048]{1,0:T(8,128)(2,1)S(1)} %get-tuple-element.26), channel_id=1, source_target_pairs={{0,4},{4,0},{8,12},{12,8},{16,20},{20,16},{24,28},{28,24},{1,5},{5... | collective-permute-start | bytes 1572872 | tf_op jit(solution)/shard_map/ppermute | solution.py:28
  70.8 11.6 %collective-permute-start.7 = (bf16[128,1024]{1,0:T(8,128)(2,1)S(1)}, bf16[128,1024]{1,0:T(8,128)(2,1)S(1)}, u32[]{:S(2)}, u32[]{:S(2)}) collective-permute-start(bf16[128,1024]{1,0:T(8,128)(2,1)S(1)} %add_convert_fusion.3), channel_id=1, source_target_pairs={{0,16},{4,20},{8,24},{12,28},{16,0},{20,4},{24,8},{28,12},{1,17},{... | collective-permute-start | bytes 786440 | tf_op jit(solution)/shard_map/ppermute | solution.py:28
  74.6 9.7 %collective-permute-start.16 = (f32[256]{0:T(256)S(1)}, f32[256]{0:T(256)S(1)}, u32[]{:S(2)}, u32[]{:S(2)}) collective-permute-start(f32[256]{0:T(256)S(1)} %get-tuple-element.37), channel_id=1, source_target_pairs={{0,4},{4,0},{8,12},{12,8},{16,20},{20,16},{24,28},{28,24},{1,5},{5... | collective-permute-start | bytes 3080 | tf_op jit(solution)/shard_map/ppermute | solution.py:28
  (1 other events, 3.4 us)

commit v4 on v3

--- a/solution.py
+++ b/solution.py
@@ -9,7 +9,7 @@
 from jax.sharding import PartitionSpec as P
 
 LANES = 128
-PARAMS = pltpu.CompilerParams(vmem_limit_bytes=40 * 1024 * 1024)
+PARAMS = pltpu.CompilerParams(vmem_limit_bytes=32 * 1024 * 1024)
 NO_COST = pl.CostEstimate(flops=0, bytes_accessed=0, transcendentals=0)
 ANY = pl.BlockSpec(memory_space=pl.ANY)
 VMEM = pl.BlockSpec(memory_space=pltpu.VMEM)
@@ -49,6 +49,10 @@
         cost_estimate=NO_COST,
         name=name,
     )(*scalars, *operands, *large, *whole, *deps)
+
+
+def touch_kernel(pooled_ref, out_ref):
+    out_ref[...] = pooled_ref[0:8, 0:LANES].astype(jnp.float32)
 
 
 def margins_kernel(pieces, ex_ref, dir_ref, pooled_ref, out_ref, ordered_ref):
@@ -114,24 +118,34 @@
     residual_ref[...] = up - labels_ref[...].astype(jnp.float32)
 
 
-def terms_kernel(places, blocks, ex_ref, scale_ref, sampled_ref, pooled_ref, *rest):
+def terms_kernel(places, blocks, with_gradient, ex_ref, scale_ref, residual_ref, sampled_ref, pooled_ref, *rest):
     *outs, signs_ref, scale_col_ref = rest
+    row = jnp.concatenate([residual_ref[at : at + 1, :] for at in range(residual_ref.shape[0])], axis=1)
+    residual = jnp.broadcast_to(row, (8, row.shape[1])).astype(jnp.bfloat16)
     cols = pooled_ref.shape[1]
     tile = tile_of(cols, 256)
     fill_scale(scale_col_ref, scale_ref[...])
     fill_signs(signs_ref, sampled_rows(sampled_ref, ex_ref[0], blocks), ex_ref[0])
     for at in range(0, cols, tile):
         weighted = weigh(pooled_ref[:, at : at + tile], scale_col_ref[...])
-        terms = jnp.dot(signs_ref[...], weighted, preferred_element_type=jnp.float32)
-        for (row, col), out in zip(places, outs):
-            if col <= at < col + out.shape[1]:
-                out[:, at - col : at - col + tile] = terms[row : row + out.shape[0]].astype(out.dtype)
-
-
-def terms_of(name, blocks, ex_scalar, scale, sampled, pooled, places, outs, deps=()):
-    rows, block_rows = pooled.shape[0], sampled.shape[1]
+        here = [(row, col, out) for (row, col), out in zip(places, outs) if col <= at < col + out.shape[1]]
+        if here:
+            low = min(row for row, _, _ in here)
+            high = max(row + out.shape[0] for row, _, out in here)
+            terms = jnp.dot(signs_ref[low:high, :], weighted, preferred_element_type=jnp.float32)
+        for row, col, out in here:
+            out[:, at - col : at - col + tile] = terms[row - low : row - low + out.shape[0]].astype(out.dtype)
+        if with_gradient:
+            terms = jnp.dot(residual, pooled_ref[:, at : at + tile], preferred_element_type=jnp.float32)
+            outs[-1][:, at : at + tile] = terms[0:1, :]
+
+
+def terms_of(name, blocks, ex_scalar, scale, residual, sampled, pooled, places, outs, deps=(), with_gradient=False):
+    (rows, cols), block_rows = pooled.shape, sampled.shape[1]
+    if with_gradient:
+        outs = [*outs, ((1, cols), jnp.float32)]
     return call(
-        functools.partial(terms_kernel, places, blocks),
+        functools.partial(terms_kernel, places, blocks, with_gradient),
         name,
         outs,
         [
@@ -139,20 +153,12 @@
             pltpu.VMEM((rows, LANES), jnp.float32),
         ],
         scale,
+        residual,
         sampled,
         scalars=(ex_scalar,),
         large=(pooled,),
         deps=deps,
     )
-
-
-def gradient_kernel(residual_ref, pooled_ref, out_ref):
-    row = jnp.concatenate([residual_ref[at : at + 1, :] for at in range(residual_ref.shape[0])], axis=1)
-    left = jnp.broadcast_to(row, (8, row.shape[1])).astype(jnp.bfloat16)
-    tile = tile_of(pooled_ref.shape[1], 512)
-    for at in range(0, pooled_ref.shape[1], tile):
-        terms = jnp.dot(left, pooled_ref[:, at : at + tile], preferred_element_type=jnp.float32)
-        out_ref[:, at : at + tile] = terms[0:1, :]
 
 
 def finish_kernel(counts, scales, *refs):
@@ -184,6 +190,8 @@
     step_dir = direction.reshape(-1, LANES) if pieces > 1 else direction
     for bit in range(bits):
         other = swap_with(step_dir, "ex", 1 << bit)
+        if bit == min(1, bits - 1):
+            touched = call(touch_kernel, "touch", [((8, LANES), jnp.float32)], [], large=(pooled,), deps=[other])
         if pieces > 1:
             step_dir = jnp.concatenate([step_dir, other])
         else:
@@ -198,6 +206,7 @@
         step_dir if pieces > 1 else step_dir.reshape(1, cols),
         scalars=(ex_scalar,),
         large=(pooled,),
+        deps=touched,
     )
     mine, theirs = terms, jnp.zeros_like(terms)
     distance = 1
@@ -221,92 +230,103 @@
     first = order[0][:2]
     cut = cols // 2 // (2 * LANES) * (2 * LANES) or cols
     spans = [(0, cut), (cut, cols)] if cut < cols else [(0, cols)]
+    begin, end = spans[0]
     made = terms_of(
         "first_terms",
         first,
         ex_scalar,
         scale,
+        residual,
         sampled,
         pooled,
-        [(0, begin) for begin, _ in spans],
-        [((len(first) * block_rows, end - begin), jnp.bfloat16) for begin, end in spans],
-    )
-    last = made
-    arrived_first = [swap_with(x, "ex", 1) for x in made]
-
-    (part,) = call(
-        gradient_kernel,
-        "gradient",
-        [((1, cols), jnp.float32)],
-        [],
-        residual,
-        large=(pooled,),
-        deps=last[:1],
-    )
-    last = [part]
-    part = part.reshape(-1)
+        [(0, begin)],
+        [((len(first) * block_rows, end - begin), jnp.bfloat16)],
+    )
+    arrived_first = [swap_with(made[0], "ex", 1)]
 
     own, arrivals = {}, {r: [] for r in range(ex_count)}
 
-    def more(blocks, name, deps):
-        cuts = [(k, r, span) for k, r in enumerate(blocks) for span in (spans if r in parted else [(0, cols)])]
+    def more(blocks, name, deps, together=(), with_gradient=False):
+        size = len(together)
+        cuts = [(k + size, r, span) for k, r in enumerate(blocks) for span in (spans if r in parted else [(0, cols)])]
         made = terms_of(
             name,
-            blocks,
+            [*together, *blocks],
             ex_scalar,
             scale,
+            residual,
             sampled,
             pooled,
-            [(k * block_rows, begin) for k, _, (begin, _) in cuts],
-            [((block_rows, end - begin), jnp.bfloat16 if r & 1 else jnp.float32) for _, r, (begin, end) in cuts],
+            [(k * block_rows, begin) for k, _, (begin, _) in cuts]
+            + [(0, begin) for begin, _ in spans[1:] if together],
+            [((block_rows, end - begin), jnp.bfloat16 if r & 1 else jnp.float32) for _, r, (begin, end) in cuts]
+            + [((size * block_rows, end - begin), jnp.bfloat16) for begin, end in spans[1:] if together],
             deps,
+            with_gradient,
         )
         for (_, r, (begin, _)), value in zip(cuts, made):
             own.setdefault(r, {})[begin] = value
+        return made[len(cuts) :] or made
 
     second = [r ^ 1 for r in first]
     parted = second + [0]
-    more(second + order[0][2:3], "second_terms", last)
+    made = more(second, "second_terms", made, first)
+    if len(spans) > 1:
+        arrived_first.append(swap_with(made[0], "ex", 1))
+
+    def gradient_round(part, bit):
+        low = (ex_index >> bit) & 1 == 0
+        lower, upper = jnp.split(part, 2)
+        arrived = swap_with(jnp.where(low, upper, lower), "ex", 1 << bit)
+        return jnp.where(low, lower, upper), arrived
+
+    if order[0][2:3]:
+        more(order[0][2:3], "third_terms", [made[0], arrived_first[0]])
 
     for k, r in enumerate(first):
         for (begin, _), value in zip(spans, arrived_first):
             arrivals[r ^ 1].append((value[k * block_rows : (k + 1) * block_rows], begin))
 
-    def exchange(r, spans):
+    def exchange(r, spans, behind=None):
         bit = (r & -r).bit_length() - 1
         for begin, end in spans:
             total = own[r][begin] if begin in own[r] and own[r][begin].shape[1] == end - begin else own[r][0][:, begin:end]
             for value, offset in arrivals[r]:
                 if offset <= begin < offset + value.shape[1]:
                     total = total + wide(value[:, begin - offset : end - offset])
+            if behind is not None:
+                total = total + wide(behind) * 0
             last = swap_with(narrow(total), "ex", 1 << bit)
             arrivals[r ^ (1 << bit)].append((last, begin))
         return last
 
     left = [r for r in range(ex_count - 1, -1, -1) if r not in own and r not in first]
     began = second[: bits - 1] if len(spans) > 1 else []
+    ahead, part = [], None
     for at, r in enumerate(began):
         last = exchange(r, spans[:1])
+        ahead.append(last)
         now, left = (left, []) if at == len(began) - 1 else (left[:-1], left[-1:])
         if now:
-            more(now, f"terms_{at}", [last])
+            made = more(now, f"terms_{at}", [last], (), part is None)
+            part = made[-1] if part is None else part
     if left:
-        more(left, "last_terms", ())
+        made = more(left, "last_terms", (), (), part is None)
+        part = made[-1] if part is None else part
     for r in order[0]:
         if r not in first:
             exchange(r, [(0, cols)])
     for bit in range(1, bits):
         for r in order[bit]:
             if r in began:
-                exchange(r, spans[1:])
+                behind = ahead[0] if r == began[0] and ahead[0].shape[1] == cols - spans[1][0] else None
+                exchange(r, spans[1:], behind)
             else:
                 exchange(r, spans if any(x.shape[1] < cols for x, _ in arrivals[r]) else [(0, cols)])
 
+    part = part.reshape(-1)
     for bit in reversed(range(bits)):
-        low = (ex_index >> bit) & 1 == 0
-        lower, upper = jnp.split(part, 2)
-        arrived = swap_with(jnp.where(low, upper, lower), "ex", 1 << bit)
-        kept = jnp.where(low, lower, upper)
+        kept, arrived = gradient_round(part, bit)
         part = kept + arrived
     ends, counts = [], []
     for begin, end in spans:

time: 86.3 us -> 83.4 us (0.966)
  waiting for transfers between devices: 25.5 us -> 29.5 us
  starting transfers between devices: 29.6 us -> 25.9 us
  local copies, waits for them, and re-layouts: 10.2 us -> 6.8 us
    ppermute x17, waiting for transfers between devices: 25.5 us -> 29.5 us  [swap_with(): return lax.ppermute(value, axis, [(i, i ^ distance) for i in range(count)])]
    ppermute x17, starting transfers between devices: 29.6 us -> 25.9 us  [swap_with(): return lax.ppermute(value, axis, [(i, i ^ distance) for i in range(count)])]
    unnamed x16 -> x18, local copies, waits for them, and re-layouts: 10.2 us -> 6.8 us
    pallas_call x8 -> x9, Pallas kernels: 16.9 us -> 17.7 us  [call(): pl.pallas_call(lambda *refs: kernel(*refs[:used], *refs[used + len(deps):...]
  transfers between devices with their start and end apart: 17 -> 17, of which waited for: 8 -> 11; matrix products, arithmetic and copies ran while one was open for 1% -> 1% of each run, Pallas kernels for 12% -> 14%
where the time goes in v4:
time: 83.4 us; the launch traced here: 83.2 us
  waiting for transfers between devices  29.5 us (35%)
  starting transfers between devices  25.9 us (31%)
  Pallas kernels  17.7 us (21%)
  local copies, waits for them, and re-layouts  6.8 us (8%)
  other arithmetic  2.6 us (3%)
    ppermute x17, waiting for transfers between devices, swap_with(): return lax.ppermute(value, axis, [(i, i ^ distance) for i in range(count)])  29.5 us
    ppermute x17, starting transfers between devices, swap_with(): return lax.ppermute(value, axis, [(i, i ^ distance) for i in range(count)])  25.9 us
    pallas_call x9, Pallas kernels, call(): pl.pallas_call(lambda *refs: kernel(*refs[:used], *refs[used + len(deps):...  17.7 us
    unnamed x18, local copies, waits for them, and re-layouts  6.8 us
  transfers between devices with their start and end apart: 17, of which 11 were waited for; matrix products, arithmetic and copies ran while one was open for 1% of the time, Pallas kernels for 14%

profile of v4, /device:TPU:0, one launch (start us, length us, event | category | flops | bytes accessed | tf_op | source)
XLA Modules:
  0.0 83.2 jit_solution(17508330047090369442)
XLA Ops:
  0.6 3.0 %collective-permute-start = (f32[2,128]{1,0:T(2,128)}, f32[2,128]{1,0:T(2,128)S(1)}, u32[]{:S(2)}, u32[]{:S(2)}) collective-permute-start(f32[2,128]{1,0:T(2,128)} %bitcast.25), channel_id=1, source_target_pairs={{0,4},{4,0},{8,12},{12,8},{16,20},{20,16},{24,28},{28,24},{1,5},{5... | collective-permute-start | bytes 3080 | tf_op jit(solution)/shard_map/ppermute | solution.py:28
  3.6 1.8 %collective-permute-done = f32[2,128]{1,0:T(2,128)S(1)} collective-permute-done((f32[2,128]{1,0:T(2,128)}, f32[2,128]{1,0:T(2,128)S(1)}, u32[]{:S(2)}, u32[]{:S(2)}) %collective-permute-start) | collective-permute-done | bytes 1056 | tf_op jit(solution)/shard_map/ppermute | solution.py:28
  6.1 2.1 %collective-permute-start.1 = (f32[4,128]{1,0:T(4,128)S(1)}, f32[4,128]{1,0:T(4,128)S(1)}, u32[]{:S(2)}, u32[]{:S(2)}) collective-permute-start(f32[4,128]{1,0:T(4,128)S(1)} %pad_maximum_fusion.2), channel_id=1, source_target_pairs={{0,8},{4,12},{8,0},{12,4},{16,24},{20,28},{24,16},{28,20},{1,9},{5... | collective-permute-start | bytes 6152 | tf_op jit(solution)/shard_map/ppermute | solution.py:28
  8.2 1.6 %collective-permute-done.1.refs_1_ = f32[4,128]{1,0:T(4,128)S(1)} collective-permute-done((f32[4,128]{1,0:T(4,128)S(1)}, f32[4,128]{1,0:T(4,128)S(1)}, u32[]{:S(2)}, u32[]{:S(2)}) %collective-permute-start.1) | collective-permute-done | bytes 2080 | tf_op jit(solution)/shard_map/ppermute | solution.py:28
  10.4 3.0 %collective-permute-start.2 = (f32[8,128]{1,0:T(8,128)S(1)}, f32[8,128]{1,0:T(8,128)S(1)}, u32[]{:S(2)}, u32[]{:S(2)}) collective-permute-start(f32[8,128]{1,0:T(8,128)S(1)} %pad_maximum_fusion.1), channel_id=1, source_target_pairs={{0,16},{4,20},{8,24},{12,28},{16,0},{20,4},{24,8},{28,12},{1,17},{... | collective-permute-start | bytes 12296 | tf_op jit(solution)/shard_map/ppermute | solution.py:28
  13.5 3.4 %copy-done = bf16[2048,2048]{1,0:T(8,128)(2,1)S(1)} copy-done((bf16[2048,2048]{1,0:T(8,128)(2,1)S(1)}, bf16[2048,2048]{1,0:T(8,128)(2,1)}, u32[]{:S(2)}) %copy-start) | copy-done | bytes 8388632
  17.0 2.3 %margins.1 = f32[16,128]{1,0:T(8,128)S(1)} custom-call(s32[1]{0:T(128)} %bitcast.refs_0_, f32[16,128]{1,0:T(8,128)S(1)} %pad_maximum_fusion.refs_1_, bf16[2048,2048]{1,0:T(8,128)(2,1)S(1)} %copy-done, f32[8,128]{1,0:T(8,128)S(1)} %touch.1.refs_3_), custom_call_target="tpu_custom_call" | custom-call | tf_op jit(solution)/shard_map/margins/pallas_call | solution.py:42
  21.9 2.1 %collective-permute-done.4.refs_1_ = f32[16,128]{1,0:T(8,128)S(1)} collective-permute-done((f32[16,128]{1,0:T(8,128)S(1)}, f32[16,128]{1,0:T(8,128)S(1)}, u32[]{:S(2)}, u32[]{:S(2)}) %collective-permute-start.4) | collective-permute-done | bytes 8224 | tf_op jit(solution)/shard_map/ppermute | solution.py:28
  24.7 1.7 %first_terms.1.refs_5_ = bf16[256,1024]{1,0:T(8,128)(2,1)S(1)} custom-call(s32[1]{0:T(128)} %bitcast.refs_0_, f32[16,128]{1,0:T(8,128)S(1)} %get-tuple-element.19.refs_1_, f32[16,128]{1,0:T(8,128)S(1)} %get-tuple-element.20.refs_2_, s32[8,128]{1,0:T(8,128)S(1)} %bitcast.14, bf16[2048,2048]{1,0:T(8,128)(2,1)S(1)} %bitcast.13), custom_call_target="tpu_custom_call" | custom-call | tf_op jit(solution)/shard_map/first_terms/pallas_call | solution.py:42
  28.0 4.2 %second_terms.1 = (f32[128,1024]{1,0:T(8,128)S(1)}, f32[128,1024]{1,0:T(8,128)S(1)}, f32[128,1024]{1,0:T(8,128)S(1)}, f32[128,1024]{1,0:T(8,128)S(1)}, bf16[256,1024]{1,0:T(8,128)(2,1)S(1)}) custom-call(s32[1]{0:T(128)} %bitcast.refs_0_, f32[16,128]{1,0:T(8,128)S(1)} %get-tuple-element.19.refs_1_, f32[16,128]{1,0:T(8,128)S(1)} %get-tuple-element.20.refs_2_, ...), custom_call_target="tpu_custom_call" | custom-call | tf_op jit(solution)/shard_map/second_terms/pallas_call | solution.py:42
  32.8 8.6 %collective-permute-done.5.refs_6_ = bf16[256,1024]{1,0:T(8,128)(2,1)S(1)} collective-permute-done((bf16[256,1024]{1,0:T(8,128)(2,1)S(1)}, bf16[256,1024]{1,0:T(8,128)(2,1)S(1)}, u32[]{:S(2)}, u32[]{:S(2)}) %collective-permute-start.5) | collective-permute-done | bytes 524320 | tf_op jit(solution)/shard_map/ppermute | solution.py:28
  42.1 1.6 %collective-permute-start.6 = (bf16[128,1024]{1,0:T(8,128)(2,1)}, bf16[128,1024]{1,0:T(8,128)(2,1)S(1)}, u32[]{:S(2)}, u32[]{:S(2)}) collective-permute-start(bf16[128,1024]{1,0:T(8,128)(2,1)} %add_convert_fusion.2), channel_id=1, source_target_pairs={{0,8},{4,12},{8,0},{12,4},{16,24},{20,28},{24,16},{28,20},{1,9},{5... | collective-permute-start | bytes 786440 | tf_op jit(solution)/shard_map/ppermute | solution.py:28
  43.7 3.4 %copy-done.1 = bf16[2048,2048]{1,0:T(8,128)(2,1)S(1)} copy-done((bf16[2048,2048]{1,0:T(8,128)(2,1)S(1)}, bf16[2048,2048]{1,0:T(8,128)(2,1)}, u32[]{:S(2)}) %copy-start.1) | copy-done | bytes 8388632
  47.1 1.8 %third_terms.1 = bf16[128,2048]{1,0:T(8,128)(2,1)S(1)} custom-call(s32[1]{0:T(128)} %bitcast.refs_0_, f32[16,128]{1,0:T(8,128)S(1)} %get-tuple-element.19.refs_1_, f32[16,128]{1,0:T(8,128)S(1)} %get-tuple-element.20.refs_2_, s32[8,128]{1,0:T(8,128)S(1)} %bitcast.16, bf16[2048,2048]{1,0:T(8,128)(2,1)S(1)} %copy-done.1, ...), custom_call_target="tpu_custom_call" | custom-call | tf_op jit(solution)/shard_map/third_terms/pallas_call | solution.py:42
  48.9 1.6 %collective-permute-start.9 = (bf16[128,2048]{1,0:T(8,128)(2,1)S(1)}, bf16[128,2048]{1,0:T(8,128)(2,1)S(1)}, u32[]{:S(2)}, u32[]{:S(2)}) collective-permute-start(bf16[128,2048]{1,0:T(8,128)(2,1)S(1)} %third_terms.1), channel_id=1, source_target_pairs={{0,4},{4,0},{8,12},{12,8},{16,20},{20,16},{24,28},{28,24},{1,5},{5... | collective-permute-start | bytes 1572872 | tf_op jit(solution)/shard_map/ppermute | solution.py:28
  50.5 4.0 %terms_0.1 = (f32[128,2048]{1,0:T(8,128)S(1)}, bf16[128,2048]{1,0:T(8,128)(2,1)S(1)}, f32[1,2048]{1,0:T(1,128)S(1)}) custom-call(s32[1]{0:T(128)} %bitcast.refs_0_, f32[16,128]{1,0:T(8,128)S(1)} %get-tuple-element.19.refs_1_, f32[16,128]{1,0:T(8,128)S(1)} %get-tuple-element.20.refs_2_, s32[8,128]{1,0:T(8,128)S(1)} %bitcast.17, ...), custom_call_target="tpu_custom_call" | custom-call | tf_op jit(solution)/shard_map/terms_0/pallas_call | solution.py:42
  56.4 1.9 %collective-permute-start.7 = (bf16[128,1024]{1,0:T(8,128)(2,1)S(1)}, bf16[128,1024]{1,0:T(8,128)(2,1)S(1)}, u32[]{:S(2)}, u32[]{:S(2)}) collective-permute-start(bf16[128,1024]{1,0:T(8,128)(2,1)S(1)} %get-tuple-element.34), channel_id=1, source_target_pairs={{0,16},{4,20},{8,24},{12,28},{16,0},{20,4},{24,8},{28,12},{1,17},{... | collective-permute-start | bytes 786440 | tf_op jit(solution)/shard_map/ppermute | solution.py:28
  60.4 3.4 %collective-permute-done.9 = bf16[128,2048]{1,0:T(8,128)(2,1)S(1)} collective-permute-done((bf16[128,2048]{1,0:T(8,128)(2,1)S(1)}, bf16[128,2048]{1,0:T(8,128)(2,1)S(1)}, u32[]{:S(2)}, u32[]{:S(2)}) %collective-permute-start.9) | collective-permute-done | bytes 524320 | tf_op jit(solution)/shard_map/ppermute | solution.py:28
  63.9 1.6 %collective-permute-start.10 = (bf16[128,2048]{1,0:T(8,128)(2,1)S(1)}, bf16[128,2048]{1,0:T(8,128)(2,1)S(1)}, u32[]{:S(2)}, u32[]{:S(2)}) collective-permute-start(bf16[128,2048]{1,0:T(8,128)(2,1)S(1)} %add_convert_fusion), channel_id=1, source_target_pairs={{0,8},{4,12},{8,0},{12,4},{16,24},{20,28},{24,16},{28,20},{1,9},{5... | collective-permute-start | bytes 1572872 | tf_op jit(solution)/shard_map/ppermute | solution.py:28
  65.6 2.2 %collective-permute-done.12 = bf16[128,1024]{1,0:T(8,128)(2,1)S(1)} collective-permute-done((bf16[128,1024]{1,0:T(8,128)(2,1)S(1)}, bf16[128,1024]{1,0:T(8,128)(2,1)S(1)}, u32[]{:S(2)}, u32[]{:S(2)}) %collective-permute-start.12) | collective-permute-done | bytes 262176 | tf_op jit(solution)/shard_map/ppermute | solution.py:28
  67.9 3.6 %collective-permute-start.13 = (bf16[128,1024]{1,0:T(8,128)(2,1)S(1)}, bf16[128,1024]{1,0:T(8,128)(2,1)S(1)}, u32[]{:S(2)}, u32[]{:S(2)}) collective-permute-start(bf16[128,1024]{1,0:T(8,128)(2,1)S(1)} %add_convert_fusion.1), channel_id=1, source_target_pairs={{0,16},{4,20},{8,24},{12,28},{16,0},{20,4},{24,8},{28,12},{1,17},{... | collective-permute-start | bytes 786440 | tf_op jit(solution)/shard_map/ppermute | solution.py:28
  71.9 1.8 %terms_1.1 = (f32[128,1024]{1,0:T(8,128)S(1)}, f32[128,1024]{1,0:T(8,128)S(1)}) custom-call(s32[1]{0:T(128)} %bitcast.refs_0_, f32[16,128]{1,0:T(8,128)S(1)} %get-tuple-element.19.refs_1_, f32[16,128]{1,0:T(8,128)S(1)} %get-tuple-element.20.refs_2_, s32[8,128]{1,0:T(8,128)S(1)} %bitcast.18, bf16[2048,2048]{1,0:T(8,128)(2,1)S(1)} %copy-done.1, ...), custom_call_target="tpu_custom_call" | custom-call | tf_op jit(solution)/shard_map/terms_1/pallas_call | solution.py:42
  75.1 4.9 %collective-permute-done.13.refs_7_ = bf16[128,1024]{1,0:T(8,128)(2,1)S(1)} collective-permute-done((bf16[128,1024]{1,0:T(8,128)(2,1)S(1)}, bf16[128,1024]{1,0:T(8,128)(2,1)S(1)}, u32[]{:S(2)}, u32[]{:S(2)}) %collective-permute-start.13) | collective-permute-done | bytes 262176 | tf_op jit(solution)/shard_map/ppermute | solution.py:28
  80.0 1.9 %collective-permute-done.10.refs_3_.refs_6_ = bf16[128,2048]{1,0:T(8,128)(2,1)S(1)} collective-permute-done((bf16[128,2048]{1,0:T(8,128)(2,1)S(1)}, bf16[128,2048]{1,0:T(8,128)(2,1)S(1)}, u32[]{:S(2)}, u32[]{:S(2)}) %collective-permute-start.10) | collective-permute-done | bytes 524320 | tf_op jit(solution)/shard_map/ppermute | solution.py:28
  (51 shorter events, 15.0 us)
Async XLA Ops:
  0.6 16.3 %copy-start.6 = (f32[256]{0:T(256)S(1)}, f32[256]{0:T(256)}, u32[]{:S(2)}) copy-start(f32[256]{0:T(256)} %param.10) | copy-start | bytes 3076
  0.6 4.8 %collective-permute-start = (f32[2,128]{1,0:T(2,128)}, f32[2,128]{1,0:T(2,128)S(1)}, u32[]{:S(2)}, u32[]{:S(2)}) collective-permute-start(f32[2,128]{1,0:T(2,128)} %bitcast.25), channel_id=1, source_target_pairs={{0,4},{4,0},{8,12},{12,8},{16,20},{20,16},{24,28},{28,24},{1,5},{5... | collective-permute-start | bytes 3080 | tf_op jit(solution)/shard_map/ppermute | solution.py:28
  6.1 3.7 %collective-permute-start.1 = (f32[4,128]{1,0:T(4,128)S(1)}, f32[4,128]{1,0:T(4,128)S(1)}, u32[]{:S(2)}, u32[]{:S(2)}) collective-permute-start(f32[4,128]{1,0:T(4,128)S(1)} %pad_maximum_fusion.2), channel_id=1, source_target_pairs={{0,8},{4,12},{8,0},{12,4},{16,24},{20,28},{24,16},{28,20},{1,9},{5... | collective-permute-start | bytes 6152 | tf_op jit(solution)/shard_map/ppermute | solution.py:28
  10.4 6.5 %collective-permute-start.2 = (f32[8,128]{1,0:T(8,128)S(1)}, f32[8,128]{1,0:T(8,128)S(1)}, u32[]{:S(2)}, u32[]{:S(2)}) collective-permute-start(f32[8,128]{1,0:T(8,128)S(1)} %pad_maximum_fusion.1), channel_id=1, source_target_pairs={{0,16},{4,20},{8,24},{12,28},{16,0},{20,4},{24,8},{28,12},{1,17},{... | collective-permute-start | bytes 12296 | tf_op jit(solution)/shard_map/ppermute | solution.py:28
  16.9 7.2 %copy-start.3 = (f32[2048]{0:T(1024)S(1)}, f32[2048]{0:T(1024)}, u32[]{:S(2)}) copy-start(f32[2048]{0:T(1024)} %param.9) | copy-start | bytes 24580
  16.9 7.2 %copy-start.4 = (s32[2048]{0:T(1024)S(1)}, s32[2048]{0:T(1024)}, u32[]{:S(2)}) copy-start(s32[2048]{0:T(1024)} %param.7) | copy-start | bytes 24580
  16.9 7.2 %copy-start.5 = (s32[2048]{0:T(1024)S(1)}, s32[2048]{0:T(1024)}, u32[]{:S(2)}) copy-start(s32[2048]{0:T(1024)} %param.8) | copy-start | bytes 24580
  16.9 7.8 %slice-start = ((s8[8388608]{0:T(1024)(128)(4,1)}), s8[4194304]{0:T(1024)(128)(4,1)S(1)}, s32[]{:S(2)}) async-start(s8[8388608]{0:T(1024)(128)(4,1)} %bitcast.12), calls=%async_computation | async-start | bytes 8388608
  16.9 7.8 %copy-start.2 = (s32[1024]{0:T(1024)S(1)}, s32[1024]{0:T(1024)}, u32[]{:S(2)}) copy-start(s32[1024]{0:T(1024)} %param.11) | copy-start | bytes 12292
  16.9 7.8 %slice-start.1 = ((s8[8388608]{0:T(1024)(128)(4,1)}), s8[4194304]{0:T(1024)(128)(4,1)S(1)}, s32[]{:S(2)}) async-start(s8[8388608]{0:T(1024)(128)(4,1)} %bitcast.12), calls=%async_computation.1 | async-start | bytes 8388608
  19.2 1.2 %collective-permute-start.3 = (f32[16,128]{1,0:T(8,128)S(1)}, f32[16,128]{1,0:T(8,128)S(1)}, u32[]{:S(2)}, u32[]{:S(2)}) collective-permute-start(f32[16,128]{1,0:T(8,128)S(1)} %margins.1), channel_id=1, source_target_pairs={{0,1},{1,0},{2,3},{3,2},{4,5},{5,4},{6,7},{7,6},{8,9},{9,8},{10,11... | collective-permute-start | bytes 24584 | tf_op jit(solution)/shard_map/ppermute | solution.py:28
  20.4 3.7 %collective-permute-start.4 = (f32[16,128]{1,0:T(8,128)S(1)}, f32[16,128]{1,0:T(8,128)S(1)}, u32[]{:S(2)}, u32[]{:S(2)}) collective-permute-start(f32[16,128]{1,0:T(8,128)S(1)} %add.33.refs_0_), channel_id=1, source_target_pairs={{0,2},{1,3},{2,0},{3,1},{4,6},{5,7},{6,4},{7,5},{8,10},{9,11},{10,... | collective-permute-start | bytes 24584 | tf_op jit(solution)/shard_map/ppermute | solution.py:28
  26.4 14.9 %collective-permute-start.5 = (bf16[256,1024]{1,0:T(8,128)(2,1)S(1)}, bf16[256,1024]{1,0:T(8,128)(2,1)S(1)}, u32[]{:S(2)}, u32[]{:S(2)}) collective-permute-start(bf16[256,1024]{1,0:T(8,128)(2,1)S(1)} %first_terms.1.refs_5_), channel_id=1, source_target_pairs={{0,4},{4,0},{8,12},{12,8},{16,20},{20,16},{24,28},{28,24},{1,5},{5... | collective-permute-start | bytes 1572872 | tf_op jit(solution)/shard_map/ppermute | solution.py:28
  32.2 23.5 %collective-permute-start.11 = (bf16[256,1024]{1,0:T(8,128)(2,1)S(1)}, bf16[256,1024]{1,0:T(8,128)(2,1)S(1)}, u32[]{:S(2)}, u32[]{:S(2)}) collective-permute-start(bf16[256,1024]{1,0:T(8,128)(2,1)S(1)} %get-tuple-element.26.refs_5_), channel_id=1, source_target_pairs={{0,4},{4,0},{8,12},{12,8},{16,20},{20,16},{24,28},{28,24},{1,5},{5... | collective-permute-start | bytes 1572872 | tf_op jit(solution)/shard_map/ppermute | solution.py:28
  42.1 8.4 %collective-permute-start.6 = (bf16[128,1024]{1,0:T(8,128)(2,1)}, bf16[128,1024]{1,0:T(8,128)(2,1)S(1)}, u32[]{:S(2)}, u32[]{:S(2)}) collective-permute-start(bf16[128,1024]{1,0:T(8,128)(2,1)} %add_convert_fusion.2), channel_id=1, source_target_pairs={{0,8},{4,12},{8,0},{12,4},{16,24},{20,28},{24,16},{28,20},{1,9},{5... | collective-permute-start | bytes 786440 | tf_op jit(solution)/shard_map/ppermute | solution.py:28
  48.9 14.9 %collective-permute-start.9 = (bf16[128,2048]{1,0:T(8,128)(2,1)S(1)}, bf16[128,2048]{1,0:T(8,128)(2,1)S(1)}, u32[]{:S(2)}, u32[]{:S(2)}) collective-permute-start(bf16[128,2048]{1,0:T(8,128)(2,1)S(1)} %third_terms.1), channel_id=1, source_target_pairs={{0,4},{4,0},{8,12},{12,8},{16,20},{20,16},{24,28},{28,24},{1,5},{5... | collective-permute-start | bytes 1572872 | tf_op jit(solution)/shard_map/ppermute | solution.py:28
  54.5 5.0 %collective-permute-start.14 = (f32[1024]{0:T(1024)S(1)}, f32[1024]{0:T(1024)S(1)}, u32[]{:S(2)}, u32[]{:S(2)}) collective-permute-start(f32[1024]{0:T(1024)S(1)} %bitcast.29), channel_id=1, source_target_pairs={{0,16},{4,20},{8,24},{12,28},{16,0},{20,4},{24,8},{28,12},{1,17},{... | collective-permute-start | bytes 12296 | tf_op jit(solution)/shard_map/ppermute | solution.py:28
  55.8 11.9 %collective-permute-start.12 = (bf16[128,1024]{1,0:T(8,128)(2,1)S(1)}, bf16[128,1024]{1,0:T(8,128)(2,1)S(1)}, u32[]{:S(2)}, u32[]{:S(2)}) collective-permute-start(bf16[128,1024]{1,0:T(8,128)(2,1)S(1)} %get-tuple-element.33), channel_id=1, source_target_pairs={{0,8},{4,12},{8,0},{12,4},{16,24},{20,28},{24,16},{28,20},{1,9},{5... | collective-permute-start | bytes 786440 | tf_op jit(solution)/shard_map/ppermute | solution.py:28
  56.4 15.6 %collective-permute-start.7 = (bf16[128,1024]{1,0:T(8,128)(2,1)S(1)}, bf16[128,1024]{1,0:T(8,128)(2,1)S(1)}, u32[]{:S(2)}, u32[]{:S(2)}) collective-permute-start(bf16[128,1024]{1,0:T(8,128)(2,1)S(1)} %get-tuple-element.34), channel_id=1, source_target_pairs={{0,16},{4,20},{8,24},{12,28},{16,0},{20,4},{24,8},{28,12},{1,17},{... | collective-permute-start | bytes 786440 | tf_op jit(solution)/shard_map/ppermute | solution.py:28
  58.2 16.9 %collective-permute-start.8 = (bf16[128,2048]{1,0:T(8,128)(2,1)S(1)}, bf16[128,2048]{1,0:T(8,128)(2,1)S(1)}, u32[]{:S(2)}, u32[]{:S(2)}) collective-permute-start(bf16[128,2048]{1,0:T(8,128)(2,1)S(1)} %get-tuple-element.24), channel_id=1, source_target_pairs={{0,4},{4,0},{8,12},{12,8},{16,20},{20,16},{24,28},{28,24},{1,5},{5... | collective-permute-start | bytes 1572872 | tf_op jit(solution)/shard_map/ppermute | solution.py:28
  59.5 11.9 %collective-permute-start.15 = (f32[512]{0:T(512)S(1)}, f32[512]{0:T(512)S(1)}, u32[]{:S(2)}, u32[]{:S(2)}) collective-permute-start(f32[512]{0:T(512)S(1)} %slice_select_fusion), channel_id=1, source_target_pairs={{0,8},{4,12},{8,0},{12,4},{16,24},{20,28},{24,16},{28,20},{1,9},{5... | collective-permute-start | bytes 6152 | tf_op jit(solution)/shard_map/ppermute | solution.py:28
  63.9 18.1 %collective-permute-start.10 = (bf16[128,2048]{1,0:T(8,128)(2,1)S(1)}, bf16[128,2048]{1,0:T(8,128)(2,1)S(1)}, u32[]{:S(2)}, u32[]{:S(2)}) collective-permute-start(bf16[128,2048]{1,0:T(8,128)(2,1)S(1)} %add_convert_fusion), channel_id=1, source_target_pairs={{0,8},{4,12},{8,0},{12,4},{16,24},{20,28},{24,16},{28,20},{1,9},{5... | collective-permute-start | bytes 1572872 | tf_op jit(solution)/shard_map/ppermute | solution.py:28
  67.9 12.2 %collective-permute-start.13 = (bf16[128,1024]{1,0:T(8,128)(2,1)S(1)}, bf16[128,1024]{1,0:T(8,128)(2,1)S(1)}, u32[]{:S(2)}, u32[]{:S(2)}) collective-permute-start(bf16[128,1024]{1,0:T(8,128)(2,1)S(1)} %add_convert_fusion.1), channel_id=1, source_target_pairs={{0,16},{4,20},{8,24},{12,28},{16,0},{20,4},{24,8},{28,12},{1,17},{... | collective-permute-start | bytes 786440 | tf_op jit(solution)/shard_map/ppermute | solution.py:28
  71.5 3.6 %collective-permute-start.16 = (f32[256]{0:T(256)S(1)}, f32[256]{0:T(256)S(1)}, u32[]{:S(2)}, u32[]{:S(2)}) collective-permute-start(f32[256]{0:T(256)S(1)} %get-tuple-element.37), channel_id=1, source_target_pairs={{0,4},{4,0},{8,12},{12,8},{16,20},{20,16},{24,28},{28,24},{1,5},{5... | collective-permute-start | bytes 3080 | tf_op jit(solution)/shard_map/ppermute | solution.py:28
  (2 other events, 6.8 us)
